TPU v7x, 32 devices: a whole 2x2x4 slice. The times are simulated.
32 devices in a mesh: section: 4 (over x, core), dp: 4 (over z), tensor: 2 (over y).
Axes of the slice: x: 2, y: 2, z: 4, core: 2. Of those that a mesh axis runs over, the one named last changes fastest.
Arguments:
- block_inputs: bfloat16 [4, 512, 3072], P('section', ('dp', 'tensor')), may hold values from -16 to 16
- qkv_weights: bfloat16 [4, 3, 3072, 3072], P('section', None, None, ('dp', 'tensor')), may hold values from -0.109375 to 0.109375
- out_weights: bfloat16 [4, 3072, 3072], P('section', ('dp', 'tensor')), may hold values from -0.109375 to 0.109375
- norm_gain: float32 [4, 3072], P('section'), may hold values from 0.25 to 1.75
- query_key_gain: float32 [4, 2, 128], P('section'), may hold values from 1.5 to 1.75
- pool_gain: float32 [4, 3072], P('section'), may hold values from 0.25 to 1.75
- class_head: bfloat16 [4, 3072, 512], P('section'), may hold values from -0.75 to 0.75
- labels: int32 [4, 2], P('section'), may hold values from 0 to 511
Outputs:
- out_rows: bfloat16 [4, 512, 3072], P('section', ('dp', 'tensor'))
- query_key_value_gradient: bfloat16 [4, 3, 3072, 3072], P('section', None, None, ('dp', 'tensor'))
- grad_out: bfloat16 [4, 3072, 3072], P('section', ('dp', 'tensor'))
- grad_head: bfloat16 [4, 3072, 512], P('section', ('dp', 'tensor'))
- losses: float32 [4, 2], P('section')
All inputs are finite; a program needn't handle non-finite values.
Results may differ from a plain program's by a relative error of at most 0.03.
Values may be sent and summed in bfloat16 or wider, within the bound.
No kernel may reach another device: no remote copies, remote signals or barrier semaphores. Data moves between devices by JAX's collectives and lax.ppermute only.
A program may use at most 128 MiB of HBM per device.

v0:
```python
import functools
import math

import jax
import jax.numpy as jnp
from jax import lax
from jax.experimental import pallas as pl
from jax.experimental.pallas import tpu as pltpu
from jax.sharding import PartitionSpec as P

HS = 128
PATCHES = 256
GROUP = ("dp", "tensor")
HALVES = 2

epsilon = 1e-06
F32 = jnp.float32
BF16 = jnp.bfloat16
VMEM_SPEC = pl.BlockSpec(memory_space=pltpu.VMEM)
SMEM_SPEC = pl.BlockSpec(memory_space=pltpu.SMEM)


def from_behind(block, axis, distance):
    devices = range(lax.axis_size(axis))
    route = [(i - distance, i) for i in devices if i - distance in devices]
    return lax.ppermute(block, axis, route)


def shift(block, axis, distance):
    count = lax.axis_size(axis)
    return lax.ppermute(block, axis, [(i, (i + distance) % count) for i in range(count)])


def after(value, *others):
    return lax.optimization_barrier((value,) + others)[0]


def way(half):
    return 1 if half % 2 == 0 else -1


def balanced(depth, width):
    return width == 2 and depth > 2


def gather_slabs(halves):
    depth, width = lax.axis_size("dp"), lax.axis_size("tensor")
    ring = [list(halves)]
    across = [[[shift(h, "tensor", j) for h in halves] for j in range(1, width)]]
    for s in range(1, depth):
        ring.append([shift(ring[-1][h], "dp", way(h)) for h in range(HALVES)])
        if s == depth - 1 and balanced(depth, width):
            quarter = ring[s][0].shape[0] // 2
            shared = []
            for h in range(HALVES):
                own, other = ring[s][h], across[-1][0][h]
                shared.append(shift(after(own[:quarter], other), "tensor", 1))
                shared.append(shift(after(other[quarter:], own), "dp", way(h)))
            across.append([shared])
            break
        across.append(
            [
                [
                    shift(after(ring[-1][h], across[-1][j - 1][h]), "tensor", j)
                    for h in range(HALVES)
                ]
                for j in range(1, width)
            ]
        )
    return [ring[s] + [p for place in across[s] for p in place] for s in range(depth)]


def scatter_slabs(slab_term):
    depth, width = lax.axis_size("dp"), lax.axis_size("tensor")
    share = balanced(depth, width)
    running = [None] * HALVES
    along = [None] * HALVES
    last = [[None] * HALVES for _ in range(width)]
    for s in list(range(1, depth)) + [0]:
        term = slab_term(s)
        half = term.shape[0] // (width * HALVES)
        quarter = half // 2
        for h in range(HALVES):
            total = term[h * half : (h + 1) * half]
            for j in range(1, width):
                start = (j * HALVES + h) * half
                piece = term[start : start + half]
                if share and s == 1:
                    top, low = piece[:quarter].astype(BF16), piece[quarter:].astype(BF16)
                    last[j][h] = shift(top, "tensor", -j)
                    along[h] = shift(low, "dp", way(h))
                    total = jnp.concatenate(
                        [total[:quarter] + last[j][h].astype(F32), total[quarter:]], axis=0
                    )
                    continue
                if share and s == 2:
                    piece = jnp.concatenate(
                        [piece[:quarter], piece[quarter:] + along[h].astype(F32)], axis=0
                    )
                piece = piece.astype(BF16)
                if last[j][h] is not None:
                    piece = after(piece, last[j][h])
                last[j][h] = shift(piece, "tensor", -j)
                total = total + last[j][h].astype(F32)
            if running[h] is not None:
                total = total + shift(running[h], "dp", way(h)).astype(F32)
            running[h] = total if s == 0 else total.astype(BF16)
    return running


def sum_group(value):
    for axis in ("tensor", "dp"):
        count = lax.axis_size(axis)
        if count & (count - 1):
            return lax.psum(value, GROUP)
    for axis in ("tensor", "dp"):
        step = 1
        while step < lax.axis_size(axis):
            route = [(i, i ^ step) for i in range(lax.axis_size(axis))]
            value = value + lax.ppermute(value, axis, route)
            step *= 2
    return value


def norm_parts(values):
    centered = values - jnp.mean(values, axis=-1, keepdims=True)
    inverse = lax.rsqrt(jnp.mean(centered * centered, axis=-1, keepdims=True) + epsilon)
    return centered * inverse, inverse


def norm_back(grad_normed, unit_rows, inverse, gain_row):
    scaled = grad_normed * gain_row
    return inverse * (
        scaled
        - jnp.mean(scaled, axis=-1, keepdims=True)
        - unit_rows * jnp.mean(scaled * unit_rows, axis=-1, keepdims=True)
    )


def dot_nt(left, right):
    return lax.dot_general(left, right, (((1,), (1,)), ((), ())), preferred_element_type=F32)


def dot_tn(left, right):
    return lax.dot_general(left, right, (((0,), (0,)), ((), ())), preferred_element_type=F32)


def dot(left, right):
    return jnp.dot(left, right, preferred_element_type=F32)


def call(kernel, out_shape, ins, specs=None, scratch=(), flops=0, moved=1000000, limit=24):
    many = isinstance(out_shape, (tuple, list))
    return pl.pallas_call(
        kernel,
        out_shape=out_shape,
        in_specs=specs or [VMEM_SPEC] * len(ins),
        out_specs=[VMEM_SPEC] * len(out_shape) if many else VMEM_SPEC,
        scratch_shapes=list(scratch),
        compiler_params=pltpu.CompilerParams(vmem_limit_bytes=limit * 2**20),
        cost_estimate=pl.CostEstimate(flops=flops, bytes_accessed=moved, transcendentals=0),
    )(*ins)


def piece_rows(local_count, depth, width):
    half = local_count // HALVES
    z, y = lax.axis_index("dp"), lax.axis_index("tensor")
    out = []
    for s in range(depth):
        for j in range(width):
            for h in range(HALVES):
                far_z = lax.rem(z + (depth - s if way(h) > 0 else s), depth)
                far_y = lax.rem(y + width - j, width)
                first = (far_z * width + far_y) * local_count + h * half
                out.append(
                    (((s * width + j) * HALVES + h) * half, pl.multiple_of(first, half), half)
                )
    return out


def to_section_order(slabs, held, pieces):
    rows = held.shape[-2] // len(slabs)
    for ring, first, count in pieces:
        s, r = divmod(ring, rows)
        if len(held.shape) == 3:
            held[:, pl.ds(first, count), :] = slabs[s][:, r : r + count, :].astype(held.dtype)
        else:
            held[pl.ds(first, count), :] = slabs[s][r : r + count, :].astype(held.dtype)


def to_ring_order(held, out, pieces):
    for ring, first, count in pieces:
        if len(held.shape) == 3:
            out[:, ring : ring + count, :] = held[:, pl.ds(first, count), :].astype(out.dtype)
        else:
            out[ring : ring + count, :] = held[pl.ds(first, count), :].astype(out.dtype)


def head_forward(held, gains, rows, lanes):
    query_unit, query_inverse = norm_parts(held[0, rows, lanes])
    key_unit, key_inverse = norm_parts(held[1, rows, lanes])
    query_half = (query_unit * gains[0:1, :]).astype(BF16)
    key_half = (key_unit * gains[1:2, :]).astype(BF16)
    value_half = held[2, rows, lanes].astype(BF16)
    exponent = jnp.exp(dot_nt(query_half, key_half) * (1.0 / math.sqrt(HS)))
    probs = exponent * (1.0 / jnp.sum(exponent, axis=-1, keepdims=True))
    return (
        probs,
        probs.astype(BF16),
        query_half,
        key_half,
        value_half,
        query_unit,
        query_inverse,
        key_unit,
        key_inverse,
    )


def each_head(held):
    row_count, lane_count = held.shape[-2:]
    for image in range(row_count // PATCHES):
        for head in range(lane_count // HS):
            yield (
                image,
                slice(image * PATCHES, (image + 1) * PATCHES),
                slice(head * HS, (head + 1) * HS),
            )


def attend_own_kernel(local_count, depth, width, *refs):
    slabs, gain_ref, out_ref, held, mixed = refs[:depth], *refs[depth:]
    pieces = piece_rows(local_count, depth, width)
    to_section_order(slabs, held, pieces)
    gains = gain_ref[...]
    for _, rows, lanes in each_head(held):
        state = head_forward(held, gains, rows, lanes)
        mixed[rows, lanes] = dot(state[1], state[4]).astype(BF16)
    to_ring_order(mixed, out_ref, pieces)


def attend_margin_kernel(local_count, depth, width, *refs):
    slabs = refs[:depth]
    gain_ref, out_weight_ref, select_ref = refs[depth : depth + 3]
    rows = refs[depth + 3 : depth + 3 + HALVES]
    sums_ref, pooled_ref, held = refs[depth + 3 + HALVES :]
    select = select_ref[...]
    rows_own = jnp.concatenate([ref[...] for ref in rows], axis=0).astype(F32)
    for image in range(select.shape[1]):
        pooled_ref[image : image + 1, :] = jnp.sum(
            rows_own * select[:, image : image + 1], axis=0, keepdims=True
        )
    pieces = piece_rows(local_count, depth, width)
    to_section_order(slabs, held, pieces)
    gains = gain_ref[...]
    for image, rows, lanes in each_head(held):
        state = head_forward(held, gains, rows, lanes)
        mixed = dot(state[1], state[4]).astype(BF16)
        sums_ref[image : image + 1, lanes] = jnp.sum(mixed.astype(F32), axis=0, keepdims=True)
    sums = sums_ref[...]
    high = sums.astype(BF16)
    rest = sums - high.astype(F32)
    middle = rest.astype(BF16)
    low = (rest - middle.astype(F32)).astype(BF16)
    weights = out_weight_ref[...]
    pooled_ref[...] = pooled_ref[...] + (
        dot(high, weights) + (dot(middle, weights) + dot(low, weights))
    )


def attend_back_kernel(local_count, depth, width, broadcast, *refs):
    slabs = refs[:depth]
    grads = refs[depth : depth + (1 if broadcast else depth)]
    gain_ref, out_ref, held, *grad_held = refs[depth + len(grads) :]
    pieces = piece_rows(local_count, depth, width)
    to_section_order(slabs, held, pieces)
    if not broadcast:
        to_section_order(grads, grad_held[0], pieces)
    gains = gain_ref[...]
    for image, rows, lanes in each_head(held):
        (
            probs,
            probs_half,
            query_half,
            key_half,
            value_half,
            query_unit,
            query_inverse,
            key_unit,
            key_inverse,
        ) = head_forward(held, gains, rows, lanes)
        if broadcast:
            row = grads[0][image : image + 1, lanes].astype(BF16).astype(F32)
            grad_mixed = jnp.broadcast_to(row, (PATCHES, HS)).astype(BF16)
        else:
            grad_mixed = grad_held[0][rows, lanes].astype(BF16)
        grad_probs = dot_nt(grad_mixed, value_half)
        grad_value = dot_tn(probs_half, grad_mixed)
        weighted = probs * grad_probs
        grad_scores = weighted - probs * jnp.sum(weighted, axis=-1, keepdims=True)
        score_half = (grad_scores * (1.0 / math.sqrt(HS))).astype(BF16)
        grad_query = dot(score_half, key_half)
        grad_key = dot_tn(score_half, query_half)
        held[0, rows, lanes] = norm_back(grad_query, query_unit, query_inverse, gains[0:1, :])
        held[1, rows, lanes] = norm_back(grad_key, key_unit, key_inverse, gains[1:2, :])
        held[2, rows, lanes] = grad_value
    to_ring_order(held, out_ref, pieces)


def project_kernel(*refs):
    weights_ref, projected_ref, turned_ref = refs[-3:]
    rows = jnp.concatenate([ref[...] for ref in refs[:-3]], axis=0)
    for t in range(weights_ref.shape[0]):
        projected_ref[t, :, :] = dot(rows, weights_ref[t])
    turned_ref[...] = rows.T


def cotangent_kernel(*refs):
    weights_ref, out_ref = refs[-2:]
    rows = jnp.concatenate([ref[...] for ref in refs[:-2]], axis=0)
    out_ref[...] = dot_nt(rows, weights_ref[...])


def input_kernel(first, count, gradient_ref, weights_ref, out_ref):
    rows = slice(first, first + count)
    total = dot_nt(gradient_ref[0, rows, :], weights_ref[0])
    for t in range(1, weights_ref.shape[0]):
        total = total + dot_nt(gradient_ref[t, rows, :], weights_ref[t])
    out_ref[...] = total


def weight_gradient_kernel(depth, *refs):
    turned = jnp.concatenate([ref[...] for ref in refs[:depth]], axis=1)
    gradient_ref, *added, out_ref = refs[depth:]
    for t in range(gradient_ref.shape[0]):
        total = dot(turned, gradient_ref[t])
        if added:
            total = total + added[0][t].astype(F32)
        out_ref[t, :, :] = total.astype(BF16)


def out_gradient_kernel(*refs):
    attention_ref, sums_ref, grad_image_ref, out_ref = refs[-4:]
    cotangent = jnp.concatenate([ref[...] for ref in refs[:-4]], axis=0)
    total = dot_tn(attention_ref[...], cotangent)
    sums = sums_ref[...]
    grad_image = grad_image_ref[...].astype(BF16).astype(F32)
    for image in range(sums.shape[1]):
        total = total + sums[:, image : image + 1] * grad_image[image : image + 1, :]
    out_ref[...] = total.astype(BF16)


def norm_rows_kernel(rows_ref, gain_ref, out_ref):
    unit_rows, _ = norm_parts(rows_ref[...].astype(F32))
    out_ref[...] = (unit_rows * gain_ref[...]).astype(BF16)


def judge_kernel(
    patch_count,
    pooled_ref,
    gain_ref,
    head_ref,
    label_ref,
    out_weight_ref,
    loss_ref,
    pooled_half_ref,
    grad_logits_ref,
    grad_image_ref,
    per_image_ref,
):
    image_count = pooled_ref.shape[0]
    unit_rows, inverse = norm_parts(pooled_ref[...] * (1.0 / patch_count))
    gain_row = gain_ref[...]
    pooled_half = (unit_rows * gain_row).astype(BF16)
    pooled_half_ref[...] = pooled_half
    head = head_ref[...]
    logits = dot(pooled_half, head)
    classes = lax.broadcasted_iota(jnp.int32, logits.shape, 1)
    images = lax.broadcasted_iota(jnp.int32, logits.shape, 0)
    label = jnp.zeros_like(classes)
    for image in range(image_count):
        label = jnp.where(images == image, label_ref[image], label)
    targets = (classes == label).astype(F32)
    softplus = jnp.maximum(logits, 0.0) + jnp.log1p(jnp.exp(-jnp.abs(logits)))
    loss_ref[...] = jnp.mean(softplus - targets * logits, axis=-1, keepdims=True)
    sigmoid = 1.0 / (1.0 + jnp.exp(-logits))
    grad_logits = ((sigmoid - targets) * (1.0 / image_count)).astype(BF16)
    grad_logits_ref[...] = grad_logits
    grad_pooled = norm_back(dot_nt(grad_logits, head), unit_rows, inverse, gain_row)
    grad_image = grad_pooled * (1.0 / patch_count)
    grad_image_ref[...] = grad_image
    per_image_ref[...] = dot_nt(grad_image.astype(BF16), out_weight_ref[...])


def grad_rows_kernel(grad_ref, rows_ref, select_ref, grad_image_ref, gain_ref, out_ref):
    unit_rows, inverse = norm_parts(rows_ref[...].astype(F32))
    total = norm_back(grad_ref[...], unit_rows, inverse, gain_ref[...])
    select = select_ref[...]
    for image in range(grad_image_ref.shape[0]):
        total = total + select[:, image : image + 1] * grad_image_ref[image : image + 1, :]
    out_ref[...] = total.astype(BF16)


def on_device(
    block_inputs, qkv_weights, out_weights, norm_gain, query_key_gain, pool_gain, class_head, labels
):
    rows_in = block_inputs[0]
    qkv_local = qkv_weights[0]
    out_local = out_weights[0]
    gain_pair = query_key_gain[0]
    label_row = labels[0]
    local_count, model_width = rows_in.shape
    image_count = label_row.shape[0]
    class_count = class_head.shape[2]
    depth, width = lax.axis_size("dp"), lax.axis_size("tensor")
    group_size = depth * width
    row_count = local_count * group_size
    lane_count = qkv_local.shape[2]
    half = local_count // HALVES
    place = (local_count, depth, width)
    member = lax.axis_index(GROUP)
    image_ids = (member * local_count + lax.iota(jnp.int32, local_count)) // PATCHES
    own_select = (image_ids[:, None] == lax.iota(jnp.int32, image_count)[None, :]).astype(F32)

    def shape(dims, dtype=F32):
        return jax.ShapeDtypeStruct(dims, dtype)

    half_shape = shape((half, model_width), BF16)
    three = (3, row_count, lane_count)
    slab_rows = local_count * width
    product_flops = 2 * row_count * lane_count * PATCHES
    slab_flops = 2 * slab_rows * model_width * lane_count

    def halves_of(rows):
        return [rows[h * half : (h + 1) * half] for h in range(HALVES)]

    def norm_rows(rows):
        return call(norm_rows_kernel, half_shape, (rows, norm_gain))

    def project(slab):
        return call(
            project_kernel,
            [shape((3, slab_rows, lane_count)), shape((model_width, slab_rows), BF16)],
            (*slab, qkv_local),
            flops=3 * slab_flops,
        )

    def weight_gradient(turned, gradient, *added):
        chunk = PATCHES * 2 if model_width % (PATCHES * 2) == 0 else PATCHES
        block = pl.BlockSpec((3, chunk, lane_count), lambda i: (0, i, 0))
        return pl.pallas_call(
            functools.partial(weight_gradient_kernel, depth),
            grid=(model_width // chunk,),
            out_shape=shape((3, model_width, lane_count), BF16),
            in_specs=[pl.BlockSpec((chunk, slab_rows), lambda i: (i, 0))] * depth
            + [pl.BlockSpec(three, lambda i: (0, 0, 0))]
            + [block] * len(added),
            out_specs=block,
            compiler_params=pltpu.CompilerParams(vmem_limit_bytes=24 * 2**20),
            cost_estimate=pl.CostEstimate(
                flops=3 * depth * slab_flops,
                bytes_accessed=6 * model_width * lane_count,
                transcendentals=0,
            ),
        )(*turned, gradient, *added)

    own_slabs = gather_slabs([norm_rows(rows) for rows in halves_of(rows_in)])
    own_projected, own_turned = zip(*[project(slab) for slab in own_slabs])
    attention = call(
        functools.partial(attend_own_kernel, *place),
        shape((row_count, lane_count), BF16),
        (*own_projected, gain_pair),
        scratch=[pltpu.VMEM(three, F32), pltpu.VMEM(three[1:], BF16)],
        flops=2 * product_flops,
    )

    def out_term(s):
        return dot(attention[s * slab_rows : (s + 1) * slab_rows], out_local)

    out_halves = [
        (rows.astype(F32) + branch).astype(BF16)
        for rows, branch in zip(halves_of(rows_in), scatter_slabs(out_term))
    ]

    first = lax.axis_index("section") == 0
    margin_halves = [
        jnp.where(first, rows, from_behind(out, "section", 1))
        for rows, out in zip(halves_of(rows_in), out_halves)
    ]
    margin_slabs = gather_slabs([norm_rows(rows) for rows in margin_halves])
    margin_projected, margin_turned = zip(*[project(slab) for slab in margin_slabs])
    image_sums, pooled_part = call(
        functools.partial(attend_margin_kernel, *place),
        [shape((image_count, lane_count)), shape((image_count, model_width))],
        (*margin_projected, gain_pair, out_local, own_select, *margin_halves),
        scratch=[pltpu.VMEM(three, F32)],
        flops=2 * product_flops,
    )
    pooled = sum_group(pooled_part)
    losses, pooled_half, grad_logits, grad_image, per_image = call(
        functools.partial(judge_kernel, PATCHES),
        [
            shape((image_count, 1)),
            shape((image_count, model_width), BF16),
            shape((image_count, class_count), BF16),
            shape((image_count, model_width)),
            shape((image_count, lane_count)),
        ],
        (pooled, pool_gain, class_head[0], label_row, out_local),
        specs=[VMEM_SPEC] * 3 + [SMEM_SPEC, VMEM_SPEC],
        flops=4 * class_count * model_width * 8,
    )
    slice_width = model_width // group_size
    pooled_slice = lax.dynamic_slice_in_dim(pooled_half, member * slice_width, slice_width, 1)
    grad_head = jnp.einsum("id,ic->dc", pooled_slice, grad_logits, preferred_element_type=F32)

    margin_gradient = call(
        functools.partial(attend_back_kernel, *place, True),
        shape(three, BF16),
        (*margin_projected, per_image, gain_pair),
        scratch=[pltpu.VMEM(three, F32)],
        flops=7 * product_flops,
    )

    def input_term(s):
        return call(
            functools.partial(input_kernel, s * slab_rows, slab_rows),
            shape((slab_rows, model_width)),
            (margin_gradient, qkv_local),
            flops=3 * slab_flops,
        )

    grad_normed = scatter_slabs(input_term)
    grad_inputs = [
        call(grad_rows_kernel, half_shape, (grad, rows, select, grad_image, norm_gain))
        for grad, rows, select in zip(grad_normed, margin_halves, halves_of(own_select))
    ]
    grad_qkv_margin = weight_gradient(margin_turned, margin_gradient)

    returned = [from_behind(grad, "section", -1) for grad in grad_inputs]
    cotangent_slabs = gather_slabs(returned)
    grad_attention = [
        call(
            cotangent_kernel,
            shape((slab_rows, lane_count)),
            (*slab, out_local),
            flops=slab_flops,
        )
        for slab in cotangent_slabs
    ]
    own_gradient = call(
        functools.partial(attend_back_kernel, *place, False),
        shape(three, BF16),
        (*own_projected, *grad_attention, gain_pair),
        scratch=[pltpu.VMEM(three, F32), pltpu.VMEM(three[1:], F32)],
        flops=7 * product_flops,
    )
    query_key_value_gradient = weight_gradient(own_turned, own_gradient, grad_qkv_margin)
    pieces = [piece for slab in cotangent_slabs for piece in slab]
    chunk = 2 * PATCHES if model_width % (2 * PATCHES) == 0 else PATCHES
    grad_out = pl.pallas_call(
        out_gradient_kernel,
        grid=(model_width // chunk,),
        out_shape=shape((lane_count, model_width), BF16),
        in_specs=[pl.BlockSpec((piece.shape[0], chunk), lambda i: (0, i)) for piece in pieces]
        + [
            pl.BlockSpec((row_count, lane_count), lambda i: (0, 0)),
            pl.BlockSpec((lane_count, image_count), lambda i: (0, 0)),
            pl.BlockSpec((image_count, chunk), lambda i: (0, i)),
        ],
        out_specs=pl.BlockSpec((lane_count, chunk), lambda i: (0, i)),
        compiler_params=pltpu.CompilerParams(vmem_limit_bytes=24 * 2**20),
        cost_estimate=pl.CostEstimate(
            flops=depth * slab_flops,
            bytes_accessed=4 * model_width * lane_count,
            transcendentals=0,
        ),
    )(*pieces, attention, image_sums.T, grad_image)
    return (
        jnp.concatenate(out_halves, axis=0)[None],
        query_key_value_gradient[None],
        grad_out[None],
        grad_head.astype(BF16)[None],
        losses.reshape(1, image_count),
    )


def solution(mesh):
    in_specs = (
        P("section", GROUP, None),
        P("section", None, None, GROUP),
        P("section", GROUP, None),
        P("section", None),
        P("section", None, None),
        P("section", None),
        P("section", None, None),
        P("section", None),
    )
    out_specs = (
        P("section", GROUP, None),
        P("section", None, None, GROUP),
        P("section", GROUP, None),
        P("section", GROUP, None),
        P("section", None),
    )
    return jax.shard_map(
        on_device, mesh=mesh, in_specs=in_specs, out_specs=out_specs, check_vma=False
    )
```

profile of v0, /device:TPU:0, one launch (start us, length us, event | category | flops | bytes accessed | tf_op | source)
XLA Modules:
  0.0 334.2 jit_solution(11068064028103753837)
XLA Ops:
  2.7 3.1 collective-permute-start.2
  10.2 3.3 collective-permute-done.2.refs_0_
  31.2 3.0 copy-done
  37.4 3.7 %collective-permute-start.15 = (bf16[16,3072]{1,0:T(8,128)(2,1)S(1)}, bf16[16,3072]{1,0:T(8,128)(2,1)S(1)}, u32[]{:S(2)}, u32[]{:S(2)}) collective-permute-start(bf16[16,3072]{1,0:T(8,128)(2,1)S(1)} %slice.331), channel_id=1, source_target_pairs={{0,6},{2,0},{4,2},{6,4},{1,7},{3,1},{5,3},{7,5},{8,14},{10,8},{12,... | collective-permute-start | bytes 294920 | tf_op jit(solution)/shard_map/ppermute | solution.py:31
  53.4 3.7 %collective-permute-start.24 = (bf16[16,3072]{1,0:T(8,128)(2,1)S(1)}, bf16[16,3072]{1,0:T(8,128)(2,1)S(1)}, u32[]{:S(2)}, u32[]{:S(2)}) collective-permute-start(bf16[16,3072]{1,0:T(8,128)(2,1)S(1)} %get-tuple-element.164), channel_id=1, source_target_pairs={{0,6},{2,0},{4,2},{6,4},{1,7},{3,1},{5,3},{7,5},{8,14},{10,8},{12,... | collective-permute-start | bytes 294920 | tf_op jit(solution)/shard_map/ppermute | solution.py:31
  58.7 3.1 collective-permute-done.17
  62.5 13.9 %collective-permute-start.21 = (bf16[32,3072]{1,0:T(8,128)(2,1)S(1)}, bf16[32,3072]{1,0:T(8,128)(2,1)S(1)}, u32[]{:S(2)}, u32[]{:S(2)}) collective-permute-start(bf16[32,3072]{1,0:T(8,128)(2,1)S(1)} %pad_maximum_fusion.1), channel_id=1, source_target_pairs={{0,2},{2,4},{4,6},{6,0},{1,3},{3,5},{5,7},{7,1},{8,10},{10,12},{12... | collective-permute-start | bytes 589832 | tf_op jit(solution)/shard_map/ppermute | solution.py:31
  79.1 5.1 %collective-permute-done.21 = bf16[32,3072]{1,0:T(8,128)(2,1)S(1)} collective-permute-done((bf16[32,3072]{1,0:T(8,128)(2,1)S(1)}, bf16[32,3072]{1,0:T(8,128)(2,1)S(1)}, u32[]{:S(2)}, u32[]{:S(2)}) %collective-permute-start.21) | collective-permute-done | bytes 196640 | tf_op jit(solution)/shard_map/ppermute | solution.py:31
  95.5 4.1 %collective-permute-done.30 = bf16[32,3072]{1,0:T(8,128)(2,1)S(1)} collective-permute-done((bf16[32,3072]{1,0:T(8,128)(2,1)S(1)}, bf16[32,3072]{1,0:T(8,128)(2,1)S(1)}, u32[]{:S(2)}, u32[]{:S(2)}) %collective-permute-start.30) | collective-permute-done | bytes 196640 | tf_op jit(solution)/shard_map/ppermute | solution.py:31
  102.3 3.8 %collective-permute-start.31 = (bf16[32,3072]{1,0:T(8,128)(2,1)S(1)}, bf16[32,3072]{1,0:T(8,128)(2,1)S(1)}, u32[]{:S(2)}, u32[]{:S(2)}) collective-permute-start(bf16[32,3072]{1,0:T(8,128)(2,1)S(1)} %get-tuple-element.136), channel_id=1, source_target_pairs={{0,6},{2,0},{4,2},{6,4},{1,7},{3,1},{5,3},{7,5},{8,14},{10,8},{12,... | collective-permute-start | bytes 589832 | tf_op jit(solution)/shard_map/ppermute | solution.py:31
  115.4 3.9 %collective-permute-start.33 = (bf16[32,3072]{1,0:T(8,128)(2,1)S(1)}, bf16[32,3072]{1,0:T(8,128)(2,1)S(1)}, u32[]{:S(2)}, u32[]{:S(2)}) collective-permute-start(bf16[32,3072]{1,0:T(8,128)(2,1)S(1)} %get-tuple-element.124), channel_id=1, source_target_pairs={{0,8},{8,16},{16,24},{1,9},{9,17},{17,25},{2,10},{10,18},{18,26},{... | collective-permute-start | bytes 589832 | tf_op jit(solution)/shard_map/ppermute | solution.py:26
  123.1 3.8 %collective-permute-start.37 = (bf16[32,3072]{1,0:T(8,128)(2,1)S(1)}, bf16[32,3072]{1,0:T(8,128)(2,1)S(1)}, u32[]{:S(2)}, u32[]{:S(2)}) collective-permute-start(bf16[32,3072]{1,0:T(8,128)(2,1)S(1)} %shard_map.127.refs_1_), channel_id=1, source_target_pairs={{0,6},{2,0},{4,2},{6,4},{1,7},{3,1},{5,3},{7,5},{8,14},{10,8},{12,... | collective-permute-start | bytes 589832 | tf_op jit(solution)/shard_map/ppermute | solution.py:31
  142.2 4.1 %collective-permute-done.41.refs_1_ = bf16[32,3072]{1,0:T(8,128)(2,1)} collective-permute-done((bf16[32,3072]{1,0:T(8,128)(2,1)S(1)}, bf16[32,3072]{1,0:T(8,128)(2,1)}, u32[]{:S(2)}, u32[]{:S(2)}) %collective-permute-start.41) | collective-permute-done | bytes 196640 | tf_op jit(solution)/shard_map/ppermute | solution.py:31
  147.0 3.6 %collective-permute-start.45 = (bf16[32,3072]{1,0:T(8,128)(2,1)}, bf16[32,3072]{1,0:T(8,128)(2,1)S(1)}, u32[]{:S(2)}, u32[]{:S(2)}) collective-permute-start(bf16[32,3072]{1,0:T(8,128)(2,1)} %collective-permute-done.41.refs_1_), channel_id=1, source_target_pairs={{0,6},{2,0},{4,2},{6,4},{1,7},{3,1},{5,3},{7,5},{8,14},{10,8},{12,... | collective-permute-start | bytes 589832 | tf_op jit(solution)/shard_map/ppermute | solution.py:31
  159.7 3.8 %collective-permute-start.49 = (bf16[16,3072]{1,0:T(8,128)(2,1)S(1)}, bf16[16,3072]{1,0:T(8,128)(2,1)S(1)}, u32[]{:S(2)}, u32[]{:S(2)}) collective-permute-start(bf16[16,3072]{1,0:T(8,128)(2,1)S(1)} %slice.361), channel_id=1, source_target_pairs={{0,6},{2,0},{4,2},{6,4},{1,7},{3,1},{5,3},{7,5},{8,14},{10,8},{12,... | collective-permute-start | bytes 294920 | tf_op jit(solution)/shard_map/ppermute | solution.py:31
  179.9 3.8 %collective-permute-done.51 = f32[2,3072]{1,0:T(2,128)S(1)} collective-permute-done((f32[2,3072]{1,0:T(2,128)S(1)}, f32[2,3072]{1,0:T(2,128)S(1)}, u32[]{:S(2)}, u32[]{:S(2)}) %collective-permute-start.51) | collective-permute-done | bytes 24608 | tf_op jit(solution)/shard_map/ppermute | solution.py:120
  183.8 4.7 %collective-permute-done.52 = f32[2,3072]{1,0:T(2,128)S(1)} collective-permute-done((f32[2,3072]{1,0:T(2,128)S(1)}, f32[2,3072]{1,0:T(2,128)S(1)}, u32[]{:S(2)}, u32[]{:S(2)}) %collective-permute-start.52) | collective-permute-done | bytes 24608 | tf_op jit(solution)/shard_map/ppermute | solution.py:120
  188.6 3.3 shard_map.133
  191.9 4.5 %shard_map.134.gradient_ref.refs_4_ = bf16[3,512,384]{2,1,0:T(8,128)(2,1)S(1)} custom-call(f32[3,128,384]{2,1,0:T(8,128)S(1)} %get-tuple-element.86.refs_0_, f32[3,128,384]{2,1,0:T(8,128)S(1)} %get-tuple-element.89.refs_1_, f32[3,128,384]{2,1,0:T(8,128)S(1)} %get-tuple-element.92.refs_2_, f32[3,128,384]{2,1,0:T(8,128)S(1)} %get-tuple-element.97.refs_3_, ...), custom_call_target="tpu_custom_call" | custom-call | flops 704643072 | bytes 1000000 | tf_op jit(solution)/shard_map/pallas_call | solution.py:154
  213.5 3.9 %collective-permute-start.67 = (bf16[32,3072]{1,0:T(8,128)(2,1)S(1)}, bf16[32,3072]{1,0:T(8,128)(2,1)S(1)}, u32[]{:S(2)}, u32[]{:S(2)}) collective-permute-start(bf16[32,3072]{1,0:T(8,128)(2,1)S(1)} %pad_maximum_fusion.7), channel_id=1, source_target_pairs={{0,6},{2,0},{4,2},{6,4},{1,7},{3,1},{5,3},{7,5},{8,14},{10,8},{12,... | collective-permute-start | bytes 589832 | tf_op jit(solution)/shard_map/ppermute | solution.py:31
  223.6 3.7 %collective-permute-start.68 = (bf16[32,3072]{1,0:T(8,128)(2,1)S(1)}, bf16[32,3072]{1,0:T(8,128)(2,1)S(1)}, u32[]{:S(2)}, u32[]{:S(2)}) collective-permute-start(bf16[32,3072]{1,0:T(8,128)(2,1)S(1)} %get-tuple-element.129), channel_id=1, source_target_pairs={{0,6},{2,0},{4,2},{6,4},{1,7},{3,1},{5,3},{7,5},{8,14},{10,8},{12,... | collective-permute-start | bytes 589832 | tf_op jit(solution)/shard_map/ppermute | solution.py:31
  232.2 3.0 collective-permute-done.59
  236.6 3.6 %collective-permute-start.69 = (bf16[32,3072]{1,0:T(8,128)(2,1)S(1)}, bf16[32,3072]{1,0:T(8,128)(2,1)S(1)}, u32[]{:S(2)}, u32[]{:S(2)}) collective-permute-start(bf16[32,3072]{1,0:T(8,128)(2,1)S(1)} %get-tuple-element.127), channel_id=1, source_target_pairs={{0,6},{2,0},{4,2},{6,4},{1,7},{3,1},{5,3},{7,5},{8,14},{10,8},{12,... | collective-permute-start | bytes 589832 | tf_op jit(solution)/shard_map/ppermute | solution.py:31
  243.5 4.2 %collective-permute-done.60 = bf16[32,3072]{1,0:T(8,128)(2,1)S(1)} collective-permute-done((bf16[32,3072]{1,0:T(8,128)(2,1)S(1)}, bf16[32,3072]{1,0:T(8,128)(2,1)S(1)}, u32[]{:S(2)}, u32[]{:S(2)}) %collective-permute-start.60) | collective-permute-done | bytes 196640 | tf_op jit(solution)/shard_map/ppermute | solution.py:31
  252.1 3.8 %collective-permute-start.74 = (bf16[32,3072]{1,0:T(8,128)(2,1)}, bf16[32,3072]{1,0:T(8,128)(2,1)}, u32[]{:S(2)}, u32[]{:S(2)}) collective-permute-start(bf16[32,3072]{1,0:T(8,128)(2,1)} %collective-permute-done.70.refs_1_), channel_id=1, source_target_pairs={{0,6},{2,0},{4,2},{6,4},{1,7},{3,1},{5,3},{7,5},{8,14},{10,8},{12,... | collective-permute-start | bytes 589832 | tf_op jit(solution)/shard_map/ppermute | solution.py:31
  258.0 3.2 collective-permute-done.74.refs_1_.refs_5_
  277.7 4.1 %collective-permute-done.77.refs_0_.refs_8_ = bf16[32,3072]{1,0:T(8,128)(2,1)} collective-permute-done((bf16[32,3072]{1,0:T(8,128)(2,1)}, bf16[32,3072]{1,0:T(8,128)(2,1)}, u32[]{:S(2)}, u32[]{:S(2)}) %collective-permute-start.77) | collective-permute-done | bytes 196640 | tf_op jit(solution)/shard_map/ppermute | solution.py:31
  288.8 6.6 %shard_map.146.refs_5_ = bf16[3,3072,384]{2,1,0:T(8,128)(2,1)S(1)} custom-call(bf16[3072,128]{1,0:T(8,128)(2,1)S(1)} %copy-done.58, bf16[3072,128]{1,0:T(8,128)(2,1)S(1)} %copy-done.60, bf16[3072,128]{1,0:T(8,128)(2,1)S(1)} %copy-done.62, bf16[3072,128]{1,0:T(8,128)(2,1)S(1)} %copy-done.64, bf16[3,512,384]{2,1,0:T(8,128)(2,1)S(1)} %shard_map.134.gradient_ref.refs_4_), custom_call_target="tpu_custom_call" | custom-call | flops 3623878656 | bytes 7077888 | tf_op jit(solution)/shard_map/pallas_call | solution.py:451
  299.1 3.5 %collective-permute-start.86 = (bf16[16,3072]{1,0:T(8,128)(2,1)S(1)}, bf16[16,3072]{1,0:T(8,128)(2,1)S(1)}, u32[]{:S(2)}, u32[]{:S(2)}) collective-permute-start(bf16[16,3072]{1,0:T(8,128)(2,1)S(1)} %slice.389), channel_id=1, source_target_pairs={{0,6},{2,0},{4,2},{6,4},{1,7},{3,1},{5,3},{7,5},{8,14},{10,8},{12,... | collective-permute-start | bytes 294920 | tf_op jit(solution)/shard_map/ppermute | solution.py:31
  316.1 4.2 %shard_map.145.refs_4_ = bf16[3,512,384]{2,1,0:T(8,128)(2,1)S(1)} custom-call(f32[3,128,384]{2,1,0:T(8,128)S(1)} %copy-done.13, f32[3,128,384]{2,1,0:T(8,128)S(1)} %copy-done.15, f32[3,128,384]{2,1,0:T(8,128)S(1)} %copy-done.17, f32[3,128,384]{2,1,0:T(8,128)S(1)} %copy-done.19, f32[128,384]{1,0:T(8,128)S(1)} %shard_map.141.refs_4_, ...), custom_call_target="tpu_custom_call" | custom-call | flops 704643072 | bytes 1000000 | tf_op jit(solution)/shard_map/pallas_call | solution.py:154
  320.4 7.8 %shard_map.147 = bf16[3,3072,384]{2,1,0:T(8,128)(2,1)} custom-call(bf16[3072,128]{1,0:T(8,128)(2,1)S(1)} %copy-done.29, bf16[3072,128]{1,0:T(8,128)(2,1)S(1)} %copy-done.31, bf16[3072,128]{1,0:T(8,128)(2,1)S(1)} %copy-done.33, bf16[3072,128]{1,0:T(8,128)(2,1)S(1)} %copy-done.35, bf16[3,512,384]{2,1,0:T(8,128)(2,1)S(1)} %shard_map.145.refs_4_, ...), custom_call_target="tpu_custom_call" | custom-call | flops 3623878656 | bytes 7077888 | tf_op jit(solution)/shard_map/pallas_call | solution.py:451
  328.2 5.7 %shard_map.148 = bf16[384,3072]{1,0:T(8,128)(2,1)} custom-call(bf16[32,3072]{1,0:T(8,128)(2,1)} %collective-permute-done.61.refs_0_, bf16[32,3072]{1,0:T(8,128)(2,1)} %collective-permute-done.70.refs_1_, bf16[32,3072]{1,0:T(8,128)(2,1)} %collective-permute-done.71.refs_2_, bf16[32,3072]{1,0:T(8,128)(2,1)} %collective-permute-done.72.refs_3_, ...), custom_call_target="tpu_custom_call" | custom-call | flops 1207959552 | bytes 4718592 | tf_op jit(solution)/shard_map/pallas_call | solution.py:561
  (376 shorter events, 192.2 us)
Async XLA Ops:
  2.7 10.8 %collective-permute-start.2 = (bf16[32,3072]{1,0:T(8,128)(2,1)S(1)}, bf16[32,3072]{1,0:T(8,128)(2,1)S(1)}, u32[]{:S(2)}, u32[]{:S(2)}) collective-permute-start(bf16[32,3072]{1,0:T(8,128)(2,1)S(1)} %shard_map.119.refs_0_), channel_id=1, source_target_pairs={{0,2},{2,4},{4,6},{6,0},{1,3},{3,5},{5,7},{7,1},{8,10},{10,12},{12... | collective-permute-start | bytes 589832 | tf_op jit(solution)/shard_map/ppermute | solution.py:31
  17.7 10.2 %collective-permute-start.7 = (bf16[32,3072]{1,0:T(8,128)(2,1)S(1)}, bf16[32,3072]{1,0:T(8,128)(2,1)S(1)}, u32[]{:S(2)}, u32[]{:S(2)}) collective-permute-start(bf16[32,3072]{1,0:T(8,128)(2,1)S(1)} %collective-permute-done.3.refs_1_), channel_id=1, source_target_pairs={{0,6},{2,0},{4,2},{6,4},{1,7},{3,1},{5,3},{7,5},{8,14},{10,8},{12,... | collective-permute-start | bytes 589832 | tf_op jit(solution)/shard_map/ppermute | solution.py:31
  23.2 13.4 %collective-permute-start.10 = (bf16[32,3072]{1,0:T(8,128)(2,1)S(1)}, bf16[32,3072]{1,0:T(8,128)(2,1)S(1)}, u32[]{:S(2)}, u32[]{:S(2)}) collective-permute-start(bf16[32,3072]{1,0:T(8,128)(2,1)S(1)} %collective-permute-done.6.refs_0_), channel_id=1, source_target_pairs={{0,2},{2,4},{4,6},{6,0},{1,3},{3,5},{5,7},{7,1},{8,10},{10,12},{12... | collective-permute-start | bytes 589832 | tf_op jit(solution)/shard_map/ppermute | solution.py:31
  24.1 12.5 %collective-permute-start.8 = (bf16[32,3072]{1,0:T(8,128)(2,1)S(1)}, bf16[32,3072]{1,0:T(8,128)(2,1)S(1)}, u32[]{:S(2)}, u32[]{:S(2)}) collective-permute-start(bf16[32,3072]{1,0:T(8,128)(2,1)S(1)} %collective-permute-done.6.refs_0_), channel_id=1, source_target_pairs={{0,1},{1,0},{2,3},{3,2},{4,5},{5,4},{6,7},{7,6},{8,9},{9,8},{10,11... | collective-permute-start | bytes 589832 | tf_op jit(solution)/shard_map/ppermute | solution.py:31
  36.6 10.7 %collective-permute-start.13 = (bf16[16,3072]{1,0:T(8,128)(2,1)S(1)}, bf16[16,3072]{1,0:T(8,128)(2,1)S(1)}, u32[]{:S(2)}, u32[]{:S(2)}) collective-permute-start(bf16[16,3072]{1,0:T(8,128)(2,1)S(1)} %slice.329), channel_id=1, source_target_pairs={{0,2},{2,4},{4,6},{6,0},{1,3},{3,5},{5,7},{7,1},{8,10},{10,12},{12... | collective-permute-start | bytes 294920 | tf_op jit(solution)/shard_map/ppermute | solution.py:31
  36.8 10.5 %collective-permute-start.12 = (bf16[16,3072]{1,0:T(8,128)(2,1)S(1)}, bf16[16,3072]{1,0:T(8,128)(2,1)S(1)}, u32[]{:S(2)}, u32[]{:S(2)}) collective-permute-start(bf16[16,3072]{1,0:T(8,128)(2,1)S(1)} %slice.328), channel_id=1, source_target_pairs={{0,1},{1,0},{2,3},{3,2},{4,5},{5,4},{6,7},{7,6},{8,9},{9,8},{10,11... | collective-permute-start | bytes 294920 | tf_op jit(solution)/shard_map/ppermute | solution.py:31
  52.8 23.6 %collective-permute-start.16 = (bf16[16,3072]{1,0:T(8,128)(2,1)S(1)}, bf16[16,3072]{1,0:T(8,128)(2,1)S(1)}, u32[]{:S(2)}, u32[]{:S(2)}) collective-permute-start(bf16[16,3072]{1,0:T(8,128)(2,1)S(1)} %get-tuple-element.161), channel_id=1, source_target_pairs={{0,2},{2,4},{4,6},{6,0},{1,3},{3,5},{5,7},{7,1},{8,10},{10,12},{12... | collective-permute-start | bytes 294920 | tf_op jit(solution)/shard_map/ppermute | solution.py:31
  53.4 22.9 %collective-permute-start.24 = (bf16[16,3072]{1,0:T(8,128)(2,1)S(1)}, bf16[16,3072]{1,0:T(8,128)(2,1)S(1)}, u32[]{:S(2)}, u32[]{:S(2)}) collective-permute-start(bf16[16,3072]{1,0:T(8,128)(2,1)S(1)} %get-tuple-element.164), channel_id=1, source_target_pairs={{0,6},{2,0},{4,2},{6,4},{1,7},{3,1},{5,3},{7,5},{8,14},{10,8},{12,... | collective-permute-start | bytes 294920 | tf_op jit(solution)/shard_map/ppermute | solution.py:31
  61.9 17.2 %collective-permute-start.29 = (bf16[32,3072]{1,0:T(8,128)(2,1)S(1)}, bf16[32,3072]{1,0:T(8,128)(2,1)S(1)}, u32[]{:S(2)}, u32[]{:S(2)}) collective-permute-start(bf16[32,3072]{1,0:T(8,128)(2,1)S(1)} %pad_maximum_fusion.3), channel_id=1, source_target_pairs={{0,6},{2,0},{4,2},{6,4},{1,7},{3,1},{5,3},{7,5},{8,14},{10,8},{12,... | collective-permute-start | bytes 589832 | tf_op jit(solution)/shard_map/ppermute | solution.py:31
  62.5 21.8 %collective-permute-start.21 = (bf16[32,3072]{1,0:T(8,128)(2,1)S(1)}, bf16[32,3072]{1,0:T(8,128)(2,1)S(1)}, u32[]{:S(2)}, u32[]{:S(2)}) collective-permute-start(bf16[32,3072]{1,0:T(8,128)(2,1)S(1)} %pad_maximum_fusion.1), channel_id=1, source_target_pairs={{0,2},{2,4},{4,6},{6,0},{1,3},{3,5},{5,7},{7,1},{8,10},{10,12},{12... | collective-permute-start | bytes 589832 | tf_op jit(solution)/shard_map/ppermute | solution.py:31
  88.3 11.3 %collective-permute-start.30 = (bf16[32,3072]{1,0:T(8,128)(2,1)S(1)}, bf16[32,3072]{1,0:T(8,128)(2,1)S(1)}, u32[]{:S(2)}, u32[]{:S(2)}) collective-permute-start(bf16[32,3072]{1,0:T(8,128)(2,1)S(1)} %get-tuple-element.138), channel_id=1, source_target_pairs={{0,6},{2,0},{4,2},{6,4},{1,7},{3,1},{5,3},{7,5},{8,14},{10,8},{12,... | collective-permute-start | bytes 589832 | tf_op jit(solution)/shard_map/ppermute | solution.py:31
  123.1 11.5 %collective-permute-start.37 = (bf16[32,3072]{1,0:T(8,128)(2,1)S(1)}, bf16[32,3072]{1,0:T(8,128)(2,1)S(1)}, u32[]{:S(2)}, u32[]{:S(2)}) collective-permute-start(bf16[32,3072]{1,0:T(8,128)(2,1)S(1)} %shard_map.127.refs_1_), channel_id=1, source_target_pairs={{0,6},{2,0},{4,2},{6,4},{1,7},{3,1},{5,3},{7,5},{8,14},{10,8},{12,... | collective-permute-start | bytes 589832 | tf_op jit(solution)/shard_map/ppermute | solution.py:31
  130.5 11.8 %collective-permute-start.38 = (bf16[32,3072]{1,0:T(8,128)(2,1)S(1)}, bf16[32,3072]{1,0:T(8,128)(2,1)}, u32[]{:S(2)}, u32[]{:S(2)}) collective-permute-start(bf16[32,3072]{1,0:T(8,128)(2,1)S(1)} %collective-permute-done.36.refs_0_), channel_id=1, source_target_pairs={{0,1},{1,0},{2,3},{3,2},{4,5},{5,4},{6,7},{7,6},{8,9},{9,8},{10,11... | collective-permute-start | bytes 589832 | tf_op jit(solution)/shard_map/ppermute | solution.py:31
  135.4 10.9 %collective-permute-start.41 = (bf16[32,3072]{1,0:T(8,128)(2,1)S(1)}, bf16[32,3072]{1,0:T(8,128)(2,1)}, u32[]{:S(2)}, u32[]{:S(2)}) collective-permute-start(bf16[32,3072]{1,0:T(8,128)(2,1)S(1)} %collective-permute-done.37.refs_1_), channel_id=1, source_target_pairs={{0,6},{2,0},{4,2},{6,4},{1,7},{3,1},{5,3},{7,5},{8,14},{10,8},{12,... | collective-permute-start | bytes 589832 | tf_op jit(solution)/shard_map/ppermute | solution.py:31
  142.2 15.6 %collective-permute-start.42 = (bf16[32,3072]{1,0:T(8,128)(2,1)}, bf16[32,3072]{1,0:T(8,128)(2,1)S(1)}, u32[]{:S(2)}, u32[]{:S(2)}) collective-permute-start(bf16[32,3072]{1,0:T(8,128)(2,1)} %collective-permute-done.40.refs_0_), channel_id=1, source_target_pairs={{0,1},{1,0},{2,3},{3,2},{4,5},{5,4},{6,7},{7,6},{8,9},{9,8},{10,11... | collective-permute-start | bytes 589832 | tf_op jit(solution)/shard_map/ppermute | solution.py:31
  146.3 13.3 %collective-permute-start.43 = (bf16[32,3072]{1,0:T(8,128)(2,1)}, bf16[32,3072]{1,0:T(8,128)(2,1)S(1)}, u32[]{:S(2)}, u32[]{:S(2)}) collective-permute-start(bf16[32,3072]{1,0:T(8,128)(2,1)} %collective-permute-done.41.refs_1_), channel_id=1, source_target_pairs={{0,1},{1,0},{2,3},{3,2},{4,5},{5,4},{6,7},{7,6},{8,9},{9,8},{10,11... | collective-permute-start | bytes 589832 | tf_op jit(solution)/shard_map/ppermute | solution.py:31
  146.8 11.1 %collective-permute-start.44 = (bf16[32,3072]{1,0:T(8,128)(2,1)}, bf16[32,3072]{1,0:T(8,128)(2,1)S(1)}, u32[]{:S(2)}, u32[]{:S(2)}) collective-permute-start(bf16[32,3072]{1,0:T(8,128)(2,1)} %collective-permute-done.40.refs_0_), channel_id=1, source_target_pairs={{0,2},{2,4},{4,6},{6,0},{1,3},{3,5},{5,7},{7,1},{8,10},{10,12},{12... | collective-permute-start | bytes 589832 | tf_op jit(solution)/shard_map/ppermute | solution.py:31
  147.0 12.7 %collective-permute-start.45 = (bf16[32,3072]{1,0:T(8,128)(2,1)}, bf16[32,3072]{1,0:T(8,128)(2,1)S(1)}, u32[]{:S(2)}, u32[]{:S(2)}) collective-permute-start(bf16[32,3072]{1,0:T(8,128)(2,1)} %collective-permute-done.41.refs_1_), channel_id=1, source_target_pairs={{0,6},{2,0},{4,2},{6,4},{1,7},{3,1},{5,3},{7,5},{8,14},{10,8},{12,... | collective-permute-start | bytes 589832 | tf_op jit(solution)/shard_map/ppermute | solution.py:31
  157.9 12.8 %collective-permute-start.47 = (bf16[16,3072]{1,0:T(8,128)(2,1)S(1)}, bf16[16,3072]{1,0:T(8,128)(2,1)S(1)}, u32[]{:S(2)}, u32[]{:S(2)}) collective-permute-start(bf16[16,3072]{1,0:T(8,128)(2,1)S(1)} %slice.359), channel_id=1, source_target_pairs={{0,2},{2,4},{4,6},{6,0},{1,3},{3,5},{5,7},{7,1},{8,10},{10,12},{12... | collective-permute-start | bytes 294920 | tf_op jit(solution)/shard_map/ppermute | solution.py:31
  158.0 12.7 %collective-permute-start.46 = (bf16[16,3072]{1,0:T(8,128)(2,1)S(1)}, bf16[16,3072]{1,0:T(8,128)(2,1)S(1)}, u32[]{:S(2)}, u32[]{:S(2)}) collective-permute-start(bf16[16,3072]{1,0:T(8,128)(2,1)S(1)} %slice.358), channel_id=1, source_target_pairs={{0,1},{1,0},{2,3},{3,2},{4,5},{5,4},{6,7},{7,6},{8,9},{9,8},{10,11... | collective-permute-start | bytes 294920 | tf_op jit(solution)/shard_map/ppermute | solution.py:31
  159.7 11.0 %collective-permute-start.49 = (bf16[16,3072]{1,0:T(8,128)(2,1)S(1)}, bf16[16,3072]{1,0:T(8,128)(2,1)S(1)}, u32[]{:S(2)}, u32[]{:S(2)}) collective-permute-start(bf16[16,3072]{1,0:T(8,128)(2,1)S(1)} %slice.361), channel_id=1, source_target_pairs={{0,6},{2,0},{4,2},{6,4},{1,7},{3,1},{5,3},{7,5},{8,14},{10,8},{12,... | collective-permute-start | bytes 294920 | tf_op jit(solution)/shard_map/ppermute | solution.py:31
  257.4 10.6 %collective-permute-start.71 = (bf16[32,3072]{1,0:T(8,128)(2,1)}, bf16[32,3072]{1,0:T(8,128)(2,1)}, u32[]{:S(2)}, u32[]{:S(2)}) collective-permute-start(bf16[32,3072]{1,0:T(8,128)(2,1)} %collective-permute-done.61.refs_0_), channel_id=1, source_target_pairs={{0,1},{1,0},{2,3},{3,2},{4,5},{5,4},{6,7},{7,6},{8,9},{9,8},{10,11... | collective-permute-start | bytes 589832 | tf_op jit(solution)/shard_map/ppermute | solution.py:31
  263.8 13.3 %collective-permute-start.76 = (bf16[32,3072]{1,0:T(8,128)(2,1)}, bf16[32,3072]{1,0:T(8,128)(2,1)}, u32[]{:S(2)}, u32[]{:S(2)}) collective-permute-start(bf16[32,3072]{1,0:T(8,128)(2,1)} %collective-permute-done.74.refs_1_.refs_5_), channel_id=1, source_target_pairs={{0,1},{1,0},{2,3},{3,2},{4,5},{5,4},{6,7},{7,6},{8,9},{9,8},{10,11... | collective-permute-start | bytes 589832 | tf_op jit(solution)/shard_map/ppermute | solution.py:31
  268.0 13.7 %collective-permute-start.75 = (bf16[32,3072]{1,0:T(8,128)(2,1)}, bf16[32,3072]{1,0:T(8,128)(2,1)}, u32[]{:S(2)}, u32[]{:S(2)}) collective-permute-start(bf16[32,3072]{1,0:T(8,128)(2,1)} %collective-permute-done.73.refs_0_.refs_4_), channel_id=1, source_target_pairs={{0,1},{1,0},{2,3},{3,2},{4,5},{5,4},{6,7},{7,6},{8,9},{9,8},{10,11... | collective-permute-start | bytes 589832 | tf_op jit(solution)/shard_map/ppermute | solution.py:31
  271.5 10.2 %collective-permute-start.77 = (bf16[32,3072]{1,0:T(8,128)(2,1)}, bf16[32,3072]{1,0:T(8,128)(2,1)}, u32[]{:S(2)}, u32[]{:S(2)}) collective-permute-start(bf16[32,3072]{1,0:T(8,128)(2,1)} %collective-permute-done.73.refs_0_.refs_4_), channel_id=1, source_target_pairs={{0,2},{2,4},{4,6},{6,0},{1,3},{3,5},{5,7},{7,1},{8,10},{10,12},{12... | collective-permute-start | bytes 589832 | tf_op jit(solution)/shard_map/ppermute | solution.py:31
  277.1 21.2 %collective-permute-start.80 = (bf16[32,3072]{1,0:T(8,128)(2,1)}, bf16[32,3072]{1,0:T(8,128)(2,1)S(1)}, u32[]{:S(2)}, u32[]{:S(2)}) collective-permute-start(bf16[32,3072]{1,0:T(8,128)(2,1)} %collective-permute-done.78.refs_1_.refs_9_), channel_id=1, source_target_pairs={{0,1},{1,0},{2,3},{3,2},{4,5},{5,4},{6,7},{7,6},{8,9},{9,8},{10,11... | collective-permute-start | bytes 589832 | tf_op jit(solution)/shard_map/ppermute | solution.py:31
  281.7 22.5 %collective-permute-start.79 = (bf16[32,3072]{1,0:T(8,128)(2,1)}, bf16[32,3072]{1,0:T(8,128)(2,1)S(1)}, u32[]{:S(2)}, u32[]{:S(2)}) collective-permute-start(bf16[32,3072]{1,0:T(8,128)(2,1)} %collective-permute-done.77.refs_0_.refs_8_), channel_id=1, source_target_pairs={{0,1},{1,0},{2,3},{3,2},{4,5},{5,4},{6,7},{7,6},{8,9},{9,8},{10,11... | collective-permute-start | bytes 589832 | tf_op jit(solution)/shard_map/ppermute | solution.py:31
  282.2 16.1 %collective-permute-start.82 = (bf16[32,3072]{1,0:T(8,128)(2,1)}, bf16[32,3072]{1,0:T(8,128)(2,1)S(1)}, u32[]{:S(2)}, u32[]{:S(2)}) collective-permute-start(bf16[32,3072]{1,0:T(8,128)(2,1)} %collective-permute-done.78.refs_1_.refs_9_), channel_id=1, source_target_pairs={{0,6},{2,0},{4,2},{6,4},{1,7},{3,1},{5,3},{7,5},{8,14},{10,8},{12,... | collective-permute-start | bytes 589832 | tf_op jit(solution)/shard_map/ppermute | solution.py:31
  284.0 20.2 %collective-permute-start.81 = (bf16[32,3072]{1,0:T(8,128)(2,1)}, bf16[32,3072]{1,0:T(8,128)(2,1)S(1)}, u32[]{:S(2)}, u32[]{:S(2)}) collective-permute-start(bf16[32,3072]{1,0:T(8,128)(2,1)} %collective-permute-done.77.refs_0_.refs_8_), channel_id=1, source_target_pairs={{0,2},{2,4},{4,6},{6,0},{1,3},{3,5},{5,7},{7,1},{8,10},{10,12},{12... | collective-permute-start | bytes 589832 | tf_op jit(solution)/shard_map/ppermute | solution.py:31
  299.1 16.0 %collective-permute-start.86 = (bf16[16,3072]{1,0:T(8,128)(2,1)S(1)}, bf16[16,3072]{1,0:T(8,128)(2,1)S(1)}, u32[]{:S(2)}, u32[]{:S(2)}) collective-permute-start(bf16[16,3072]{1,0:T(8,128)(2,1)S(1)} %slice.389), channel_id=1, source_target_pairs={{0,6},{2,0},{4,2},{6,4},{1,7},{3,1},{5,3},{7,5},{8,14},{10,8},{12,... | collective-permute-start | bytes 294920 | tf_op jit(solution)/shard_map/ppermute | solution.py:31
  302.7 12.5 %collective-permute-start.85 = (bf16[16,3072]{1,0:T(8,128)(2,1)S(1)}, bf16[16,3072]{1,0:T(8,128)(2,1)S(1)}, u32[]{:S(2)}, u32[]{:S(2)}) collective-permute-start(bf16[16,3072]{1,0:T(8,128)(2,1)S(1)} %slice.388), channel_id=1, source_target_pairs={{0,1},{1,0},{2,3},{3,2},{4,5},{5,4},{6,7},{7,6},{8,9},{9,8},{10,11... | collective-permute-start | bytes 294920 | tf_op jit(solution)/shard_map/ppermute | solution.py:31
  305.0 10.2 %collective-permute-start.84 = (bf16[16,3072]{1,0:T(8,128)(2,1)S(1)}, bf16[16,3072]{1,0:T(8,128)(2,1)S(1)}, u32[]{:S(2)}, u32[]{:S(2)}) collective-permute-start(bf16[16,3072]{1,0:T(8,128)(2,1)S(1)} %slice.387), channel_id=1, source_target_pairs={{0,2},{2,4},{4,6},{6,0},{1,3},{3,5},{5,7},{7,1},{8,10},{10,12},{12... | collective-permute-start | bytes 294920 | tf_op jit(solution)/shard_map/ppermute | solution.py:31
  (127 other events, 967.1 us)
where the time goes:
time: 338 us; the launch traced here: 334 us
  starting transfers between devices  132 us (39%)
  waiting for transfers between devices  92.6 us (27%)
  Pallas kernels  68.7 us (20%)
  local copies, waits for them, and re-layouts  29.7 us (9%)
  other arithmetic  4.69 us (1%)
  matrix products  4.05 us (1%)
    ppermute x80, starting transfers between devices, shift(): lax.ppermute(block, axis, [(i, (i + distance) % count) for i in range(cou...  123 us
    ppermute x80, waiting for transfers between devices, shift(): lax.ppermute(block, axis, [(i, (i + distance) % count) for i in range(cou...  80.5 us
    pallas_call x27, Pallas kernels, call(): pl.pallas_call(kernel, out_shape=out_shape, in_specs=specs or [VMEM_SPEC]...  48.6 us
    unnamed x144, local copies, waits for them, and re-layouts  26.9 us
    pallas_call x2, Pallas kernels, weight_gradient(): pl.pallas_call(functools.partial(weight_gradient_kernel, depth), grid=(mo...  14.4 us
    ppermute x3, waiting for transfers between devices, sum_group(): value = value + lax.ppermute(value, axis, route)  10.8 us
    ppermute x4, starting transfers between devices, from_behind(): return lax.ppermute(block, axis, route)  7.78 us
  transfers between devices with their start and end apart: 87, of which 43 were waited for; matrix products, arithmetic and copies ran while one was open for 2% of the time, Pallas kernels for 9%

commit v1 on v0

--- a/solution.py
+++ b/solution.py
@@ -39,65 +39,36 @@
     return 1 if half % 2 == 0 else -1
 
 
-def balanced(depth, width):
-    return width == 2 and depth > 2
-
-
-def gather_slabs(halves):
+def gather_slabs(halves, work):
     depth, width = lax.axis_size("dp"), lax.axis_size("tensor")
-    ring = [list(halves)]
-    across = [[[shift(h, "tensor", j) for h in halves] for j in range(1, width)]]
-    for s in range(1, depth):
-        ring.append([shift(ring[-1][h], "dp", way(h)) for h in range(HALVES)])
-        if s == depth - 1 and balanced(depth, width):
-            quarter = ring[s][0].shape[0] // 2
-            shared = []
+    ring, slabs, results = [list(halves)], [], []
+    across = [[None] * HALVES for _ in range(width)]
+    for s in range(depth):
+        if s:
+            ring.append([shift(ring[-1][h], "dp", way(h)) for h in range(HALVES)])
+        pieces = list(ring[s])
+        for j in range(1, width):
             for h in range(HALVES):
-                own, other = ring[s][h], across[-1][0][h]
-                shared.append(shift(after(own[:quarter], other), "tensor", 1))
-                shared.append(shift(after(other[quarter:], own), "dp", way(h)))
-            across.append([shared])
-            break
-        across.append(
-            [
-                [
-                    shift(after(ring[-1][h], across[-1][j - 1][h]), "tensor", j)
-                    for h in range(HALVES)
-                ]
-                for j in range(1, width)
-            ]
-        )
-    return [ring[s] + [p for place in across[s] for p in place] for s in range(depth)]
-
-
-def scatter_slabs(slab_term):
+                piece = ring[s][h]
+                if s:
+                    piece = after(piece, across[j][h], *results[: s - 1][-1:])
+                across[j][h] = shift(piece, "tensor", j)
+                pieces.append(across[j][h])
+        slabs.append(pieces)
+        results.append(work(s, pieces))
+    return slabs, results
+
+
+def scatter_slabs(slab_pieces):
     depth, width = lax.axis_size("dp"), lax.axis_size("tensor")
-    share = balanced(depth, width)
     running = [None] * HALVES
-    along = [None] * HALVES
     last = [[None] * HALVES for _ in range(width)]
     for s in list(range(1, depth)) + [0]:
-        term = slab_term(s)
-        half = term.shape[0] // (width * HALVES)
-        quarter = half // 2
+        terms = slab_pieces(s)
         for h in range(HALVES):
-            total = term[h * half : (h + 1) * half]
+            total = terms[h].astype(F32)
             for j in range(1, width):
-                start = (j * HALVES + h) * half
-                piece = term[start : start + half]
-                if share and s == 1:
-                    top, low = piece[:quarter].astype(BF16), piece[quarter:].astype(BF16)
-                    last[j][h] = shift(top, "tensor", -j)
-                    along[h] = shift(low, "dp", way(h))
-                    total = jnp.concatenate(
-                        [total[:quarter] + last[j][h].astype(F32), total[quarter:]], axis=0
-                    )
-                    continue
-                if share and s == 2:
-                    piece = jnp.concatenate(
-                        [piece[:quarter], piece[quarter:] + along[h].astype(F32)], axis=0
-                    )
-                piece = piece.astype(BF16)
+                piece = terms[j * HALVES + h]
                 if last[j][h] is not None:
                     piece = after(piece, last[j][h])
                 last[j][h] = shift(piece, "tensor", -j)
@@ -108,17 +79,20 @@
     return running
 
 
+def exchange(value, axis, steps):
+    route = [(i, i ^ steps) for i in range(lax.axis_size(axis))]
+    return lax.ppermute(value, axis, route)
+
+
 def sum_group(value):
-    for axis in ("tensor", "dp"):
-        count = lax.axis_size(axis)
-        if count & (count - 1):
-            return lax.psum(value, GROUP)
-    for axis in ("tensor", "dp"):
-        step = 1
-        while step < lax.axis_size(axis):
-            route = [(i, i ^ step) for i in range(lax.axis_size(axis))]
-            value = value + lax.ppermute(value, axis, route)
-            step *= 2
+    counts = [lax.axis_size(axis) for axis in ("tensor", "dp")]
+    if any(count & (count - 1) for count in counts):
+        return lax.psum(value, GROUP)
+    for axis, count in zip(("tensor", "dp"), counts):
+        parts = [value] + [exchange(value, axis, step) for step in range(1, count)]
+        while len(parts) > 1:
+            parts = [parts[i] + parts[i + 1] for i in range(0, len(parts), 2)]
+        value = parts[0]
     return value
 
 
@@ -268,51 +242,63 @@
     )
 
 
+def state_kernel(local_count, depth, width, *refs):
+    slabs = refs[:depth]
+    gain_ref, probs_ref, turned_ref, halves_ref, units_ref, inverse_ref, held = refs[depth:]
+    to_section_order(slabs, held, piece_rows(local_count, depth, width))
+    gains = gain_ref[...]
+    for place, (_, rows, lanes) in enumerate(each_head(held)):
+        head = lanes.start // HS
+        state = head_forward(held, gains, rows, lanes)
+        probs_ref[place, :, :] = state[0]
+        turned_ref[place, :, :] = state[1].T
+        for t in range(3):
+            halves_ref[t, rows, lanes] = state[2 + t]
+        for t in range(2):
+            units_ref[t, rows, lanes] = state[5 + 2 * t]
+            inverse_ref[t, rows, head : head + 1] = state[6 + 2 * t]
+
+
 def attend_back_kernel(local_count, depth, width, broadcast, *refs):
-    slabs = refs[:depth]
-    grads = refs[depth : depth + (1 if broadcast else depth)]
-    gain_ref, out_ref, held, *grad_held = refs[depth + len(grads) :]
+    probs_ref, turned_ref, halves_ref, units_ref, inverse_ref = refs[:5]
+    grads = refs[5 : 6 if broadcast else 5 + depth]
+    gain_ref, out_ref, held, *grad_held = refs[5 + len(grads) :]
     pieces = piece_rows(local_count, depth, width)
-    to_section_order(slabs, held, pieces)
     if not broadcast:
         to_section_order(grads, grad_held[0], pieces)
     gains = gain_ref[...]
-    for image, rows, lanes in each_head(held):
-        (
-            probs,
-            probs_half,
-            query_half,
-            key_half,
-            value_half,
-            query_unit,
-            query_inverse,
-            key_unit,
-            key_inverse,
-        ) = head_forward(held, gains, rows, lanes)
+    for place, (image, rows, lanes) in enumerate(each_head(held)):
+        head = lanes.start // HS
         if broadcast:
             row = grads[0][image : image + 1, lanes].astype(BF16).astype(F32)
             grad_mixed = jnp.broadcast_to(row, (PATCHES, HS)).astype(BF16)
         else:
             grad_mixed = grad_held[0][rows, lanes].astype(BF16)
-        grad_probs = dot_nt(grad_mixed, value_half)
-        grad_value = dot_tn(probs_half, grad_mixed)
+        probs = probs_ref[place]
+        grad_probs = dot_nt(grad_mixed, halves_ref[2, rows, lanes])
         weighted = probs * grad_probs
         grad_scores = weighted - probs * jnp.sum(weighted, axis=-1, keepdims=True)
         score_half = (grad_scores * (1.0 / math.sqrt(HS))).astype(BF16)
-        grad_query = dot(score_half, key_half)
-        grad_key = dot_tn(score_half, query_half)
-        held[0, rows, lanes] = norm_back(grad_query, query_unit, query_inverse, gains[0:1, :])
-        held[1, rows, lanes] = norm_back(grad_key, key_unit, key_inverse, gains[1:2, :])
-        held[2, rows, lanes] = grad_value
+        grads_out = (
+            dot(score_half, halves_ref[1, rows, lanes]),
+            dot_tn(score_half, halves_ref[0, rows, lanes]),
+        )
+        for t in range(2):
+            held[t, rows, lanes] = norm_back(
+                grads_out[t],
+                units_ref[t, rows, lanes],
+                inverse_ref[t, rows, head : head + 1],
+                gains[t : t + 1, :],
+            )
+        held[2, rows, lanes] = dot(turned_ref[place], grad_mixed)
     to_ring_order(held, out_ref, pieces)
 
 
 def project_kernel(*refs):
-    weights_ref, projected_ref, turned_ref = refs[-3:]
-    rows = jnp.concatenate([ref[...] for ref in refs[:-3]], axis=0)
+    weights_ref, projected_ref = refs[-2:]
+    rows = jnp.concatenate([ref[...] for ref in refs[:-2]], axis=0)
     for t in range(weights_ref.shape[0]):
         projected_ref[t, :, :] = dot(rows, weights_ref[t])
-    turned_ref[...] = rows.T
 
 
 def cotangent_kernel(*refs):
@@ -321,21 +307,31 @@
     out_ref[...] = dot_nt(rows, weights_ref[...])
 
 
-def input_kernel(first, count, gradient_ref, weights_ref, out_ref):
+def to_pieces(total, outs):
+    count = outs[0].shape[0]
+    for i, out in enumerate(outs):
+        out[...] = total[i * count : (i + 1) * count].astype(BF16)
+
+
+def branch_kernel(first, count, attention_ref, weights_ref, *outs):
+    to_pieces(dot(attention_ref[first : first + count, :], weights_ref[...]), outs)
+
+
+def input_kernel(first, count, gradient_ref, weights_ref, *outs):
     rows = slice(first, first + count)
     total = dot_nt(gradient_ref[0, rows, :], weights_ref[0])
     for t in range(1, weights_ref.shape[0]):
         total = total + dot_nt(gradient_ref[t, rows, :], weights_ref[t])
-    out_ref[...] = total
-
-
-def weight_gradient_kernel(depth, *refs):
-    turned = jnp.concatenate([ref[...] for ref in refs[:depth]], axis=1)
-    gradient_ref, *added, out_ref = refs[depth:]
-    for t in range(gradient_ref.shape[0]):
-        total = dot(turned, gradient_ref[t])
+    to_pieces(total, outs)
+
+
+def weight_gradient_kernel(count, first, *refs):
+    pieces, gradient_ref, added, out_ref = refs[:count], refs[count], refs[count + 1 : -1], refs[-1]
+    rows = jnp.concatenate([ref[...] for ref in pieces], axis=0)
+    for t in range(out_ref.shape[0]):
+        total = dot_tn(rows, gradient_ref[first + t])
         if added:
-            total = total + added[0][t].astype(F32)
+            total = total + added[t][0].astype(F32)
         out_ref[t, :, :] = total.astype(BF16)
 
 
@@ -344,15 +340,49 @@
     cotangent = jnp.concatenate([ref[...] for ref in refs[:-4]], axis=0)
     total = dot_tn(attention_ref[...], cotangent)
     sums = sums_ref[...]
+    image_count, lane_count = sums.shape
+    sums = jnp.concatenate([sums, jnp.zeros((-image_count % 8, lane_count), F32)], axis=0).T
     grad_image = grad_image_ref[...].astype(BF16).astype(F32)
-    for image in range(sums.shape[1]):
+    for image in range(image_count):
         total = total + sums[:, image : image + 1] * grad_image[image : image + 1, :]
     out_ref[...] = total.astype(BF16)
+
+
+def head_gradient_kernel(width, pooled_half_ref, grad_logits_ref, out_ref):
+    member = lax.axis_index("dp") * width + lax.axis_index("tensor")
+    count = out_ref.shape[0]
+    start = pl.multiple_of(member * count, HS)
+    pooled = pooled_half_ref[:, pl.ds(start, count)].astype(F32)
+    grad_logits = grad_logits_ref[...].astype(F32)
+
+    def padded(rows):
+        empty = jnp.zeros((-rows.shape[0] % 16, rows.shape[1]), F32)
+        return jnp.concatenate([rows, empty], axis=0).astype(BF16)
+
+    out_ref[...] = dot_tn(padded(pooled), padded(grad_logits)).astype(BF16)
+
+
+def join_kernel(*refs):
+    refs[-1][...] = jnp.concatenate([ref[...] for ref in refs[:-1]], axis=0)
 
 
 def norm_rows_kernel(rows_ref, gain_ref, out_ref):
     unit_rows, _ = norm_parts(rows_ref[...].astype(F32))
     out_ref[...] = (unit_rows * gain_ref[...]).astype(BF16)
+
+
+def norm_margin_kernel(first_ref, rows_ref, received_ref, gain_ref, out_ref, margin_ref):
+    first = first_ref[0] == 1
+
+    @pl.when(first)
+    def _():
+        margin_ref[...] = rows_ref[...]
+
+    @pl.when(jnp.logical_not(first))
+    def _():
+        margin_ref[...] = received_ref[...]
+
+    norm_rows_kernel(margin_ref, gain_ref, out_ref)
 
 
 def judge_kernel(
@@ -428,44 +458,64 @@
     half_shape = shape((half, model_width), BF16)
     three = (3, row_count, lane_count)
     slab_rows = local_count * width
+    heads = image_count * (lane_count // HS)
     product_flops = 2 * row_count * lane_count * PATCHES
     slab_flops = 2 * slab_rows * model_width * lane_count
+    chunk = 2 * PATCHES if model_width % (2 * PATCHES) == 0 else PATCHES
+    piece_shapes = [half_shape] * (width * HALVES)
 
     def halves_of(rows):
         return [rows[h * half : (h + 1) * half] for h in range(HALVES)]
 
-    def norm_rows(rows):
-        return call(norm_rows_kernel, half_shape, (rows, norm_gain))
-
-    def project(slab):
+    def project(_, pieces):
         return call(
             project_kernel,
-            [shape((3, slab_rows, lane_count)), shape((model_width, slab_rows), BF16)],
-            (*slab, qkv_local),
+            shape((3, slab_rows, lane_count)),
+            (*pieces, qkv_local),
             flops=3 * slab_flops,
+            limit=16,
         )
 
-    def weight_gradient(turned, gradient, *added):
-        chunk = PATCHES * 2 if model_width % (PATCHES * 2) == 0 else PATCHES
-        block = pl.BlockSpec((3, chunk, lane_count), lambda i: (0, i, 0))
+    def state_of(projected):
+        return call(
+            functools.partial(state_kernel, *place),
+            [
+                shape((heads, PATCHES, PATCHES)),
+                shape((heads, PATCHES, PATCHES), BF16),
+                shape(three, BF16),
+                shape((2, row_count, lane_count)),
+                shape((2, row_count, lane_count // HS)),
+            ],
+            (*projected, gain_pair),
+            scratch=[pltpu.VMEM(three, F32)],
+            flops=2 * product_flops,
+        )
+
+    def weight_gradient(slabs, gradient, first, count, *added):
+        pieces = [piece for slab in slabs for piece in slab]
         return pl.pallas_call(
-            functools.partial(weight_gradient_kernel, depth),
+            functools.partial(weight_gradient_kernel, len(pieces), first),
             grid=(model_width // chunk,),
-            out_shape=shape((3, model_width, lane_count), BF16),
-            in_specs=[pl.BlockSpec((chunk, slab_rows), lambda i: (i, 0))] * depth
+            out_shape=shape((count, model_width, lane_count), BF16),
+            in_specs=[pl.BlockSpec((half, chunk), lambda i: (0, i))] * len(pieces)
             + [pl.BlockSpec(three, lambda i: (0, 0, 0))]
-            + [block] * len(added),
-            out_specs=block,
-            compiler_params=pltpu.CompilerParams(vmem_limit_bytes=24 * 2**20),
+            + [pl.BlockSpec((1, chunk, lane_count), lambda i: (0, i, 0))] * len(added),
+            out_specs=pl.BlockSpec((count, chunk, lane_count), lambda i: (0, i, 0)),
+            compiler_params=pltpu.CompilerParams(vmem_limit_bytes=20 * 2**20),
             cost_estimate=pl.CostEstimate(
-                flops=3 * depth * slab_flops,
-                bytes_accessed=6 * model_width * lane_count,
+                flops=count * depth * slab_flops,
+                bytes_accessed=4 * count * model_width * lane_count,
                 transcendentals=0,
             ),
-        )(*turned, gradient, *added)
-
-    own_slabs = gather_slabs([norm_rows(rows) for rows in halves_of(rows_in)])
-    own_projected, own_turned = zip(*[project(slab) for slab in own_slabs])
+        )(*pieces, gradient, *added)
+
+    own_slabs, own_projected = gather_slabs(
+        [
+            call(norm_rows_kernel, half_shape, (rows, norm_gain), limit=4)
+            for rows in halves_of(rows_in)
+        ],
+        project,
+    )
     attention = call(
         functools.partial(attend_own_kernel, *place),
         shape((row_count, lane_count), BF16),
@@ -474,21 +524,34 @@
         flops=2 * product_flops,
     )
 
-    def out_term(s):
-        return dot(attention[s * slab_rows : (s + 1) * slab_rows], out_local)
+    def branch(s):
+        return call(
+            functools.partial(branch_kernel, s * slab_rows, slab_rows),
+            piece_shapes,
+            (attention, out_local),
+            flops=slab_flops,
+            limit=16,
+        )
 
     out_halves = [
-        (rows.astype(F32) + branch).astype(BF16)
-        for rows, branch in zip(halves_of(rows_in), scatter_slabs(out_term))
+        (rows.astype(F32) + total).astype(BF16)
+        for rows, total in zip(halves_of(rows_in), scatter_slabs(branch))
     ]
 
-    first = lax.axis_index("section") == 0
-    margin_halves = [
-        jnp.where(first, rows, from_behind(out, "section", 1))
-        for rows, out in zip(halves_of(rows_in), out_halves)
-    ]
-    margin_slabs = gather_slabs([norm_rows(rows) for rows in margin_halves])
-    margin_projected, margin_turned = zip(*[project(slab) for slab in margin_slabs])
+    first = (lax.axis_index("section") == 0).astype(jnp.int32).reshape(1)
+    margin_normed, margin_halves = zip(
+        *[
+            call(
+                norm_margin_kernel,
+                [half_shape] * 2,
+                (first, rows, from_behind(out, "section", 1), norm_gain),
+                specs=[SMEM_SPEC] + [VMEM_SPEC] * 3,
+                limit=4,
+            )
+            for rows, out in zip(halves_of(rows_in), out_halves)
+        ]
+    )
+    margin_slabs, margin_projected = gather_slabs(margin_normed, project)
     image_sums, pooled_part = call(
         functools.partial(attend_margin_kernel, *place),
         [shape((image_count, lane_count)), shape((image_count, model_width))],
@@ -496,7 +559,9 @@
         scratch=[pltpu.VMEM(three, F32)],
         flops=2 * product_flops,
     )
-    pooled = sum_group(pooled_part)
+    own_state = state_of(own_projected)
+    margin_state = state_of(margin_projected)
+    pooled = after(sum_group(pooled_part), own_state[4], margin_state[4])
     losses, pooled_half, grad_logits, grad_image, per_image = call(
         functools.partial(judge_kernel, PATCHES),
         [
@@ -509,78 +574,87 @@
         (pooled, pool_gain, class_head[0], label_row, out_local),
         specs=[VMEM_SPEC] * 3 + [SMEM_SPEC, VMEM_SPEC],
         flops=4 * class_count * model_width * 8,
-    )
-    slice_width = model_width // group_size
-    pooled_slice = lax.dynamic_slice_in_dim(pooled_half, member * slice_width, slice_width, 1)
-    grad_head = jnp.einsum("id,ic->dc", pooled_slice, grad_logits, preferred_element_type=F32)
+        limit=16,
+    )
+    grad_head = call(
+        functools.partial(head_gradient_kernel, width),
+        shape((model_width // group_size, class_count), BF16),
+        (pooled_half, grad_logits),
+        limit=4,
+    )
 
     margin_gradient = call(
         functools.partial(attend_back_kernel, *place, True),
         shape(three, BF16),
-        (*margin_projected, per_image, gain_pair),
+        (*margin_state, per_image, gain_pair),
         scratch=[pltpu.VMEM(three, F32)],
-        flops=7 * product_flops,
+        flops=5 * product_flops,
     )
 
     def input_term(s):
         return call(
             functools.partial(input_kernel, s * slab_rows, slab_rows),
-            shape((slab_rows, model_width)),
+            piece_shapes,
             (margin_gradient, qkv_local),
             flops=3 * slab_flops,
+            limit=16,
         )
 
     grad_normed = scatter_slabs(input_term)
     grad_inputs = [
-        call(grad_rows_kernel, half_shape, (grad, rows, select, grad_image, norm_gain))
+        call(grad_rows_kernel, half_shape, (grad, rows, select, grad_image, norm_gain), limit=6)
         for grad, rows, select in zip(grad_normed, margin_halves, halves_of(own_select))
     ]
-    grad_qkv_margin = weight_gradient(margin_turned, margin_gradient)
+    margin_parts = [weight_gradient(margin_slabs, margin_gradient, t, 1) for t in range(3)]
 
     returned = [from_behind(grad, "section", -1) for grad in grad_inputs]
-    cotangent_slabs = gather_slabs(returned)
-    grad_attention = [
-        call(
+
+    def cotangent(s, pieces):
+        if s < len(margin_parts):
+            pieces = [after(pieces[0], margin_parts[s])] + pieces[1:]
+        return call(
             cotangent_kernel,
             shape((slab_rows, lane_count)),
-            (*slab, out_local),
+            (*pieces, out_local),
             flops=slab_flops,
+            limit=16,
         )
-        for slab in cotangent_slabs
-    ]
+
+    cotangent_slabs, grad_attention = gather_slabs(returned, cotangent)
     own_gradient = call(
         functools.partial(attend_back_kernel, *place, False),
         shape(three, BF16),
-        (*own_projected, *grad_attention, gain_pair),
+        (*own_state, *grad_attention, gain_pair),
         scratch=[pltpu.VMEM(three, F32), pltpu.VMEM(three[1:], F32)],
-        flops=7 * product_flops,
-    )
-    query_key_value_gradient = weight_gradient(own_turned, own_gradient, grad_qkv_margin)
+        flops=5 * product_flops,
+    )
+    query_key_value_gradient = weight_gradient(own_slabs, own_gradient, 0, 3, *margin_parts)
     pieces = [piece for slab in cotangent_slabs for piece in slab]
-    chunk = 2 * PATCHES if model_width % (2 * PATCHES) == 0 else PATCHES
+    wide = 2 * chunk if model_width % (2 * chunk) == 0 else chunk
     grad_out = pl.pallas_call(
         out_gradient_kernel,
-        grid=(model_width // chunk,),
+        grid=(model_width // wide,),
         out_shape=shape((lane_count, model_width), BF16),
-        in_specs=[pl.BlockSpec((piece.shape[0], chunk), lambda i: (0, i)) for piece in pieces]
+        in_specs=[pl.BlockSpec((half, wide), lambda i: (0, i))] * len(pieces)
         + [
             pl.BlockSpec((row_count, lane_count), lambda i: (0, 0)),
-            pl.BlockSpec((lane_count, image_count), lambda i: (0, 0)),
-            pl.BlockSpec((image_count, chunk), lambda i: (0, i)),
+            pl.BlockSpec((image_count, lane_count), lambda i: (0, 0)),
+            pl.BlockSpec((image_count, wide), lambda i: (0, i)),
         ],
-        out_specs=pl.BlockSpec((lane_count, chunk), lambda i: (0, i)),
-        compiler_params=pltpu.CompilerParams(vmem_limit_bytes=24 * 2**20),
+        out_specs=pl.BlockSpec((lane_count, wide), lambda i: (0, i)),
+        compiler_params=pltpu.CompilerParams(vmem_limit_bytes=20 * 2**20),
         cost_estimate=pl.CostEstimate(
             flops=depth * slab_flops,
             bytes_accessed=4 * model_width * lane_count,
             transcendentals=0,
         ),
-    )(*pieces, attention, image_sums.T, grad_image)
+    )(*pieces, attention, image_sums, grad_image)
+    out_own = call(join_kernel, shape((local_count, model_width), BF16), tuple(out_halves), limit=4)
     return (
-        jnp.concatenate(out_halves, axis=0)[None],
+        out_own[None],
         query_key_value_gradient[None],
         grad_out[None],
-        grad_head.astype(BF16)[None],
+        grad_head[None],
         losses.reshape(1, image_count),
     )
 

time: 338 us -> 307 us (0.908)
  waiting for transfers between devices: 92.6 us -> 67.7 us
  starting transfers between devices: 132 us -> 109 us
  Pallas kernels: 68.7 us -> 82.4 us
  local copies, waits for them, and re-layouts: 29.7 us -> 36.7 us
  matrix products: 4.05 us -> 0 us
    ppermute x80 -> x70, starting transfers between devices: 123 us -> 96.1 us  [shift(): lax.ppermute(block, axis, [(i, (i + distance) % count) for i in range(cou...]
    ppermute x80 -> x70, waiting for transfers between devices: 80.5 us -> 64.4 us  [shift(): lax.ppermute(block, axis, [(i, (i + distance) % count) for i in range(cou...]
    unnamed x144 -> x270, local copies, waits for them, and re-layouts: 26.9 us -> 35.7 us
    ppermute x3 -> x4, waiting for transfers between devices: 10.8 us -> 2.65 us  [exchange(): return lax.ppermute(value, axis, route)]
    pallas_call x27 -> x35, Pallas kernels: 48.6 us -> 55.6 us  [call(): pl.pallas_call(kernel, out_shape=out_shape, in_specs=specs or [VMEM_SPEC]...]
    pallas_call x3 -> x5, Pallas kernels: 20.1 us -> 26.8 us  [the longest x4 22.1 us: weight_gradient(): pl.pallas_call(functools.partial(weight_gradient_kernel, len(pieces), fir...]
    dot_general x5 -> x0, matrix products: 4.05 us -> none  [the longest x4 2.3 us: dot(): return jnp.dot(left, right, preferred_element_type=F32)]
  transfers between devices with their start and end apart: 87 -> 78, of which waited for: 43 -> 35; matrix products, arithmetic and copies ran while one was open for 2% -> 1% of each run, Pallas kernels for 9% -> 16%
where the time goes in v1:
time: 307 us; the launch traced here: 301 us
  starting transfers between devices  109 us (36%)
  Pallas kernels  82.4 us (27%)
  waiting for transfers between devices  67.7 us (22%)
  local copies, waits for them, and re-layouts  36.7 us (12%)
    ppermute x70, starting transfers between devices, shift(): lax.ppermute(block, axis, [(i, (i + distance) % count) for i in range(cou...  96.1 us
    ppermute x70, waiting for transfers between devices, shift(): lax.ppermute(block, axis, [(i, (i + distance) % count) for i in range(cou...  64.4 us
    pallas_call x35, Pallas kernels, call(): pl.pallas_call(kernel, out_shape=out_shape, in_specs=specs or [VMEM_SPEC]...  55.6 us
    unnamed x270, local copies, waits for them, and re-layouts  35.7 us
    pallas_call x4, Pallas kernels, weight_gradient(): pl.pallas_call(functools.partial(weight_gradient_kernel, len(pieces), fir...  22.1 us
    ppermute x4, starting transfers between devices, from_behind(): return lax.ppermute(block, axis, route)  8.27 us
  transfers between devices with their start and end apart: 78, of which 35 were waited for; matrix products, arithmetic and copies ran while one was open for 1% of the time, Pallas kernels for 16%

profile of v1, /device:TPU:0, one launch (start us, length us, event | category | flops | bytes accessed | tf_op | source)
XLA Modules:
  0.0 301.2 jit_solution(1137768721638729026)
XLA Ops:
  2.7 3.0 %collective-permute-start = (bf16[32,3072]{1,0:T(8,128)(2,1)S(1)}, bf16[32,3072]{1,0:T(8,128)(2,1)S(1)}, u32[]{:S(2)}, u32[]{:S(2)}) collective-permute-start(bf16[32,3072]{1,0:T(8,128)(2,1)S(1)} %shard_map.119.refs_0_), channel_id=1, source_target_pairs={{0,1},{1,0},{2,3},{3,2},{4,5},{5,4},{6,7},{7,6},{8,9},{9,8},{10,11... | collective-permute-start | bytes 589832 | tf_op jit(solution)/shard_map/ppermute | solution.py:31
  11.5 3.9 %collective-permute-done.2.refs_0_.refs_4_ = bf16[32,3072]{1,0:T(8,128)(2,1)S(1)} collective-permute-done((bf16[32,3072]{1,0:T(8,128)(2,1)S(1)}, bf16[32,3072]{1,0:T(8,128)(2,1)S(1)}, u32[]{:S(2)}, u32[]{:S(2)}) %collective-permute-start.2) | collective-permute-done | bytes 196640 | tf_op jit(solution)/shard_map/ppermute | solution.py:31
  15.7 3.1 %collective-permute-done.3.refs_1_.refs_5_ = bf16[32,3072]{1,0:T(8,128)(2,1)S(1)} collective-permute-done((bf16[32,3072]{1,0:T(8,128)(2,1)S(1)}, bf16[32,3072]{1,0:T(8,128)(2,1)S(1)}, u32[]{:S(2)}, u32[]{:S(2)}) %collective-permute-start.3) | collective-permute-done | bytes 196640 | tf_op jit(solution)/shard_map/ppermute | solution.py:31
  18.8 2.7 collective-permute-start.7
  21.5 3.0 copy-done
  29.2 2.7 collective-permute-start.11
  52.6 3.8 %collective-permute-done.21 = bf16[32,3072]{1,0:T(8,128)(2,1)S(1)} collective-permute-done((bf16[32,3072]{1,0:T(8,128)(2,1)S(1)}, bf16[32,3072]{1,0:T(8,128)(2,1)S(1)}, u32[]{:S(2)}, u32[]{:S(2)}) %collective-permute-start.21) | collective-permute-done | bytes 196640 | tf_op jit(solution)/shard_map/ppermute | solution.py:31
  63.6 13.9 %collective-permute-start.26 = (bf16[32,3072]{1,0:T(8,128)(2,1)S(1)}, bf16[32,3072]{1,0:T(8,128)(2,1)S(1)}, u32[]{:S(2)}, u32[]{:S(2)}) collective-permute-start(bf16[32,3072]{1,0:T(8,128)(2,1)S(1)} %add_convert_fusion.8), channel_id=1, source_target_pairs={{0,6},{2,0},{4,2},{6,4},{1,7},{3,1},{5,3},{7,5},{8,14},{10,8},{12,... | collective-permute-start | bytes 589832 | tf_op jit(solution)/shard_map/ppermute | solution.py:31
  79.8 3.1 %collective-permute-done.26 = bf16[32,3072]{1,0:T(8,128)(2,1)S(1)} collective-permute-done((bf16[32,3072]{1,0:T(8,128)(2,1)S(1)}, bf16[32,3072]{1,0:T(8,128)(2,1)S(1)}, u32[]{:S(2)}, u32[]{:S(2)}) %collective-permute-start.26) | collective-permute-done | bytes 196640 | tf_op jit(solution)/shard_map/ppermute | solution.py:31
  93.0 3.5 %collective-permute-done.20 = bf16[32,3072]{1,0:T(8,128)(2,1)S(1)} collective-permute-done((bf16[32,3072]{1,0:T(8,128)(2,1)S(1)}, bf16[32,3072]{1,0:T(8,128)(2,1)S(1)}, u32[]{:S(2)}, u32[]{:S(2)}) %collective-permute-start.20) | collective-permute-done | bytes 196640 | tf_op jit(solution)/shard_map/ppermute | solution.py:31
  99.5 3.7 %collective-permute-start.29 = (bf16[32,3072]{1,0:T(8,128)(2,1)}, bf16[32,3072]{1,0:T(8,128)(2,1)}, u32[]{:S(2)}, u32[]{:S(2)}) collective-permute-start(bf16[32,3072]{1,0:T(8,128)(2,1)} %get-tuple-element.179.refs_1_), channel_id=1, source_target_pairs={{0,8},{8,16},{16,24},{1,9},{9,17},{17,25},{2,10},{10,18},{18,26},{... | collective-permute-start | bytes 589832 | tf_op jit(solution)/shard_map/ppermute | solution.py:26
  111.6 3.8 %collective-permute-start.33 = (bf16[32,3072]{1,0:T(8,128)(2,1)S(1)}, bf16[32,3072]{1,0:T(8,128)(2,1)}, u32[]{:S(2)}, u32[]{:S(2)}) collective-permute-start(bf16[32,3072]{1,0:T(8,128)(2,1)S(1)} %get-tuple-element.126.refs_1_), channel_id=1, source_target_pairs={{0,6},{2,0},{4,2},{6,4},{1,7},{3,1},{5,3},{7,5},{8,14},{10,8},{12,... | collective-permute-start | bytes 589832 | tf_op jit(solution)/shard_map/ppermute | solution.py:31
  121.6 4.4 %collective-permute-start.37 = (bf16[32,3072]{1,0:T(8,128)(2,1)}, bf16[32,3072]{1,0:T(8,128)(2,1)}, u32[]{:S(2)}, u32[]{:S(2)}) collective-permute-start(bf16[32,3072]{1,0:T(8,128)(2,1)} %collective-permute-done.33.refs_1_.refs_5_), channel_id=1, source_target_pairs={{0,6},{2,0},{4,2},{6,4},{1,7},{3,1},{5,3},{7,5},{8,14},{10,8},{12,... | collective-permute-start | bytes 589832 | tf_op jit(solution)/shard_map/ppermute | solution.py:31
  126.0 3.0 copy-done.2
  136.3 3.8 %collective-permute-start.41 = (bf16[32,3072]{1,0:T(8,128)(2,1)}, bf16[32,3072]{1,0:T(8,128)(2,1)S(1)}, u32[]{:S(2)}, u32[]{:S(2)}) collective-permute-start(bf16[32,3072]{1,0:T(8,128)(2,1)} %collective-permute-done.37.refs_1_.refs_9_), channel_id=1, source_target_pairs={{0,6},{2,0},{4,2},{6,4},{1,7},{3,1},{5,3},{7,5},{8,14},{10,8},{12,... | collective-permute-start | bytes 589832 | tf_op jit(solution)/shard_map/ppermute | solution.py:31
  153.3 2.8 shard_map.139
  157.3 2.6 collective-permute-done.44
  163.6 2.7 shard_map.131
  170.3 2.7 shard_map.138
  173.1 3.6 %shard_map.140 = (f32[2,1]{1,0:T(2,128)S(1)}, bf16[2,3072]{1,0:T(2,128)(2,1)S(1)}, bf16[2,512]{1,0:T(2,128)(2,1)S(1)}, f32[2,3072]{1,0:T(2,128)S(1)}, f32[2,384]{1,0:T(2,128)S(1)}) custom-call(f32[2,3072]{1,0:T(2,128)S(1)} %add_add_fusion.pooled_ref, f32[1,3072]{1,0:T(1,128)S(1)} %copy-done.126, bf16[3072,512]{1,0:T(8,128)(2,1)S(1)} %bitcast.43, ...), custom_call_target="tpu_custom_call" | custom-call | flops 50331648 | bytes 1000000 | tf_op jit(solution)/shard_map/pallas_call | solution.py:128
  176.8 2.8 shard_map.141.gradient_ref.refs_16_
  197.1 3.5 %collective-permute-done.52 = bf16[32,3072]{1,0:T(8,128)(2,1)S(1)} collective-permute-done((bf16[32,3072]{1,0:T(8,128)(2,1)S(1)}, bf16[32,3072]{1,0:T(8,128)(2,1)S(1)}, u32[]{:S(2)}, u32[]{:S(2)}) %collective-permute-start.52) | collective-permute-done | bytes 196640 | tf_op jit(solution)/shard_map/ppermute | solution.py:31
  201.5 3.0 collective-permute-done.60
  229.9 3.4 %collective-permute-done.66.refs_0_.refs_4_ = bf16[32,3072]{1,0:T(8,128)(2,1)S(1)} collective-permute-done((bf16[32,3072]{1,0:T(8,128)(2,1)S(1)}, bf16[32,3072]{1,0:T(8,128)(2,1)S(1)}, u32[]{:S(2)}, u32[]{:S(2)}) %collective-permute-start.66) | collective-permute-done | bytes 196640 | tf_op jit(solution)/shard_map/ppermute | solution.py:31
  234.3 3.2 %collective-permute-done.67.refs_1_.refs_5_ = bf16[32,3072]{1,0:T(8,128)(2,1)S(1)} collective-permute-done((bf16[32,3072]{1,0:T(8,128)(2,1)S(1)}, bf16[32,3072]{1,0:T(8,128)(2,1)S(1)}, u32[]{:S(2)}, u32[]{:S(2)}) %collective-permute-start.67) | collective-permute-done | bytes 196640 | tf_op jit(solution)/shard_map/ppermute | solution.py:31
  239.4 4.7 %shard_map.147.refs_17_ = bf16[1,3072,384]{2,1,0:T(8,128)(2,1)S(1)} custom-call(bf16[32,3072]{1,0:T(8,128)(2,1)S(1)} %copy-done.16, bf16[32,3072]{1,0:T(8,128)(2,1)S(1)} %copy-done.24, bf16[32,3072]{1,0:T(8,128)(2,1)S(1)} %copy-done.20, bf16[32,3072]{1,0:T(8,128)(2,1)S(1)} %copy-done.28, bf16[32,3072]{1,0:T(8,128)(2,1)} %collective-permute-done.32.refs_0_.refs_4_, ...), custom_call_target="tpu_custom_call" | custom-call | flops 1207959552 | bytes 4718592 | tf_op jit(solution)/shard_map/pallas_call | solution.py:496
  250.1 3.0 collective-permute-start.75
  253.1 4.7 %shard_map.150.refs_18_ = bf16[1,3072,384]{2,1,0:T(8,128)(2,1)S(1)} custom-call(bf16[32,3072]{1,0:T(8,128)(2,1)S(1)} %copy-done.16, bf16[32,3072]{1,0:T(8,128)(2,1)S(1)} %copy-done.24, bf16[32,3072]{1,0:T(8,128)(2,1)S(1)} %copy-done.20, bf16[32,3072]{1,0:T(8,128)(2,1)S(1)} %copy-done.28, bf16[32,3072]{1,0:T(8,128)(2,1)} %collective-permute-done.32.refs_0_.refs_4_, ...), custom_call_target="tpu_custom_call" | custom-call | flops 1207959552 | bytes 4718592 | tf_op jit(solution)/shard_map/pallas_call | solution.py:496
  277.0 4.8 %shard_map.152.refs_19_ = bf16[1,3072,384]{2,1,0:T(8,128)(2,1)S(1)} custom-call(bf16[32,3072]{1,0:T(8,128)(2,1)S(1)} %copy-done.17, bf16[32,3072]{1,0:T(8,128)(2,1)S(1)} %copy-done.25, bf16[32,3072]{1,0:T(8,128)(2,1)S(1)} %copy-done.21, bf16[32,3072]{1,0:T(8,128)(2,1)S(1)} %copy-done.29, bf16[32,3072]{1,0:T(8,128)(2,1)} %collective-permute-done.32.refs_0_.refs_4_, ...), custom_call_target="tpu_custom_call" | custom-call | flops 1207959552 | bytes 4718592 | tf_op jit(solution)/shard_map/pallas_call | solution.py:496
  285.2 2.8 shard_map.155.refs_16_
  288.3 8.0 %shard_map.156 = bf16[3,3072,384]{2,1,0:T(8,128)(2,1)} custom-call(bf16[32,3072]{1,0:T(8,128)(2,1)S(1)} %copy-done.44, bf16[32,3072]{1,0:T(8,128)(2,1)S(1)} %copy-done.46, bf16[32,3072]{1,0:T(8,128)(2,1)S(1)} %copy-done.58, bf16[32,3072]{1,0:T(8,128)(2,1)S(1)} %copy-done.62, bf16[32,3072]{1,0:T(8,128)(2,1)S(1)} %copy-done.60, ...), custom_call_target="tpu_custom_call" | custom-call | flops 3623878656 | bytes 14155776 | tf_op jit(solution)/shard_map/pallas_call | solution.py:496
  296.4 4.6 %shard_map.157 = bf16[384,3072]{1,0:T(8,128)(2,1)} custom-call(bf16[32,3072]{1,0:T(8,128)(2,1)S(1)} %copy-done.86, bf16[32,3072]{1,0:T(8,128)(2,1)S(1)} %copy-done.88, bf16[32,3072]{1,0:T(8,128)(2,1)S(1)} %copy-done.90, bf16[32,3072]{1,0:T(8,128)(2,1)S(1)} %copy-done.94, bf16[32,3072]{1,0:T(8,128)(2,1)S(1)} %copy-done.92, bf16[32,3072]{1,0:T(8,128)(2,1)S(1)} %copy-done.96, ...), custom_call_target="tpu_custom_call" | custom-call | flops 1207959552 | bytes 4718592 | tf_op jit(solution)/shard_map/pallas_call | solution.py:634
  (457 shorter events, 174.2 us)
Async XLA Ops:
  8.2 10.6 %collective-permute-start.3 = (bf16[32,3072]{1,0:T(8,128)(2,1)S(1)}, bf16[32,3072]{1,0:T(8,128)(2,1)S(1)}, u32[]{:S(2)}, u32[]{:S(2)}) collective-permute-start(bf16[32,3072]{1,0:T(8,128)(2,1)S(1)} %shard_map.120.refs_1_), channel_id=1, source_target_pairs={{0,6},{2,0},{4,2},{6,4},{1,7},{3,1},{5,3},{7,5},{8,14},{10,8},{12,... | collective-permute-start | bytes 589832 | tf_op jit(solution)/shard_map/ppermute | solution.py:31
  15.4 10.5 %collective-permute-start.4 = (bf16[32,3072]{1,0:T(8,128)(2,1)S(1)}, bf16[32,3072]{1,0:T(8,128)(2,1)S(1)}, u32[]{:S(2)}, u32[]{:S(2)}) collective-permute-start(bf16[32,3072]{1,0:T(8,128)(2,1)S(1)} %collective-permute-done.2.refs_0_.refs_4_), channel_id=1, source_target_pairs={{0,1},{1,0},{2,3},{3,2},{4,5},{5,4},{6,7},{7,6},{8,9},{9,8},{10,11... | collective-permute-start | bytes 589832 | tf_op jit(solution)/shard_map/ppermute | solution.py:31
  15.7 10.3 %collective-permute-start.6 = (bf16[32,3072]{1,0:T(8,128)(2,1)S(1)}, bf16[32,3072]{1,0:T(8,128)(2,1)S(1)}, u32[]{:S(2)}, u32[]{:S(2)}) collective-permute-start(bf16[32,3072]{1,0:T(8,128)(2,1)S(1)} %collective-permute-done.2.refs_0_.refs_4_), channel_id=1, source_target_pairs={{0,2},{2,4},{4,6},{6,0},{1,3},{3,5},{5,7},{7,1},{8,10},{10,12},{12... | collective-permute-start | bytes 589832 | tf_op jit(solution)/shard_map/ppermute | solution.py:31
  27.9 10.1 %collective-permute-start.9 = (bf16[32,3072]{1,0:T(8,128)(2,1)S(1)}, bf16[32,3072]{1,0:T(8,128)(2,1)S(1)}, u32[]{:S(2)}, u32[]{:S(2)}) collective-permute-start(bf16[32,3072]{1,0:T(8,128)(2,1)S(1)} %collective-permute-done.7.refs_1_.refs_9_), channel_id=1, source_target_pairs={{0,1},{1,0},{2,3},{3,2},{4,5},{5,4},{6,7},{7,6},{8,9},{9,8},{10,11... | collective-permute-start | bytes 589832 | tf_op jit(solution)/shard_map/ppermute | solution.py:31
  49.9 10.7 %collective-permute-start.14 = (bf16[32,3072]{1,0:T(8,128)(2,1)S(1)}, bf16[32,3072]{1,0:T(8,128)(2,1)S(1)}, u32[]{:S(2)}, u32[]{:S(2)}) collective-permute-start(bf16[32,3072]{1,0:T(8,128)(2,1)S(1)} %get-tuple-element.102), channel_id=1, source_target_pairs={{0,1},{1,0},{2,3},{3,2},{4,5},{5,4},{6,7},{7,6},{8,9},{9,8},{10,11... | collective-permute-start | bytes 589832 | tf_op jit(solution)/shard_map/ppermute | solution.py:31
  60.6 17.6 %collective-permute-start.18 = (bf16[32,3072]{1,0:T(8,128)(2,1)S(1)}, bf16[32,3072]{1,0:T(8,128)(2,1)S(1)}, u32[]{:S(2)}, u32[]{:S(2)}) collective-permute-start(bf16[32,3072]{1,0:T(8,128)(2,1)S(1)} %add_convert_fusion.13), channel_id=1, source_target_pairs={{0,2},{2,4},{4,6},{6,0},{1,3},{3,5},{5,7},{7,1},{8,10},{10,12},{12... | collective-permute-start | bytes 589832 | tf_op jit(solution)/shard_map/ppermute | solution.py:31
  60.7 17.5 %collective-permute-start.15 = (bf16[32,3072]{1,0:T(8,128)(2,1)S(1)}, bf16[32,3072]{1,0:T(8,128)(2,1)S(1)}, u32[]{:S(2)}, u32[]{:S(2)}) collective-permute-start(bf16[32,3072]{1,0:T(8,128)(2,1)S(1)} %get-tuple-element.103), channel_id=1, source_target_pairs={{0,1},{1,0},{2,3},{3,2},{4,5},{5,4},{6,7},{7,6},{8,9},{9,8},{10,11... | collective-permute-start | bytes 589832 | tf_op jit(solution)/shard_map/ppermute | solution.py:31
  63.6 19.3 %collective-permute-start.26 = (bf16[32,3072]{1,0:T(8,128)(2,1)S(1)}, bf16[32,3072]{1,0:T(8,128)(2,1)S(1)}, u32[]{:S(2)}, u32[]{:S(2)}) collective-permute-start(bf16[32,3072]{1,0:T(8,128)(2,1)S(1)} %add_convert_fusion.8), channel_id=1, source_target_pairs={{0,6},{2,0},{4,2},{6,4},{1,7},{3,1},{5,3},{7,5},{8,14},{10,8},{12,... | collective-permute-start | bytes 589832 | tf_op jit(solution)/shard_map/ppermute | solution.py:31
  78.3 10.6 %collective-permute-start.19 = (bf16[32,3072]{1,0:T(8,128)(2,1)S(1)}, bf16[32,3072]{1,0:T(8,128)(2,1)S(1)}, u32[]{:S(2)}, u32[]{:S(2)}) collective-permute-start(bf16[32,3072]{1,0:T(8,128)(2,1)S(1)} %add_convert_fusion.12), channel_id=1, source_target_pairs={{0,2},{2,4},{4,6},{6,0},{1,3},{3,5},{5,7},{7,1},{8,10},{10,12},{12... | collective-permute-start | bytes 589832 | tf_op jit(solution)/shard_map/ppermute | solution.py:31
  78.9 10.0 %collective-permute-start.16 = (bf16[32,3072]{1,0:T(8,128)(2,1)S(1)}, bf16[32,3072]{1,0:T(8,128)(2,1)S(1)}, u32[]{:S(2)}, u32[]{:S(2)}) collective-permute-start(bf16[32,3072]{1,0:T(8,128)(2,1)S(1)} %get-tuple-element.104), channel_id=1, source_target_pairs={{0,1},{1,0},{2,3},{3,2},{4,5},{5,4},{6,7},{7,6},{8,9},{9,8},{10,11... | collective-permute-start | bytes 589832 | tf_op jit(solution)/shard_map/ppermute | solution.py:31
  106.0 10.1 %collective-permute-start.30 = (bf16[32,3072]{1,0:T(8,128)(2,1)S(1)}, bf16[32,3072]{1,0:T(8,128)(2,1)S(1)}, u32[]{:S(2)}, u32[]{:S(2)}) collective-permute-start(bf16[32,3072]{1,0:T(8,128)(2,1)S(1)} %get-tuple-element.125.refs_0_), channel_id=1, source_target_pairs={{0,1},{1,0},{2,3},{3,2},{4,5},{5,4},{6,7},{7,6},{8,9},{9,8},{10,11... | collective-permute-start | bytes 589832 | tf_op jit(solution)/shard_map/ppermute | solution.py:31
  106.9 9.9 %collective-permute-start.32 = (bf16[32,3072]{1,0:T(8,128)(2,1)S(1)}, bf16[32,3072]{1,0:T(8,128)(2,1)}, u32[]{:S(2)}, u32[]{:S(2)}) collective-permute-start(bf16[32,3072]{1,0:T(8,128)(2,1)S(1)} %get-tuple-element.125.refs_0_), channel_id=1, source_target_pairs={{0,2},{2,4},{4,6},{6,0},{1,3},{3,5},{5,7},{7,1},{8,10},{10,12},{12... | collective-permute-start | bytes 589832 | tf_op jit(solution)/shard_map/ppermute | solution.py:31
  116.7 17.4 %collective-permute-start.34 = (bf16[32,3072]{1,0:T(8,128)(2,1)}, bf16[32,3072]{1,0:T(8,128)(2,1)}, u32[]{:S(2)}, u32[]{:S(2)}) collective-permute-start(bf16[32,3072]{1,0:T(8,128)(2,1)} %collective-permute-done.32.refs_0_.refs_4_), channel_id=1, source_target_pairs={{0,1},{1,0},{2,3},{3,2},{4,5},{5,4},{6,7},{7,6},{8,9},{9,8},{10,11... | collective-permute-start | bytes 589832 | tf_op jit(solution)/shard_map/ppermute | solution.py:31
  117.6 16.6 %collective-permute-start.36 = (bf16[32,3072]{1,0:T(8,128)(2,1)}, bf16[32,3072]{1,0:T(8,128)(2,1)}, u32[]{:S(2)}, u32[]{:S(2)}) collective-permute-start(bf16[32,3072]{1,0:T(8,128)(2,1)} %collective-permute-done.32.refs_0_.refs_4_), channel_id=1, source_target_pairs={{0,2},{2,4},{4,6},{6,0},{1,3},{3,5},{5,7},{7,1},{8,10},{10,12},{12... | collective-permute-start | bytes 589832 | tf_op jit(solution)/shard_map/ppermute | solution.py:31
  120.8 14.6 %collective-permute-start.35 = (bf16[32,3072]{1,0:T(8,128)(2,1)}, bf16[32,3072]{1,0:T(8,128)(2,1)}, u32[]{:S(2)}, u32[]{:S(2)}) collective-permute-start(bf16[32,3072]{1,0:T(8,128)(2,1)} %collective-permute-done.33.refs_1_.refs_5_), channel_id=1, source_target_pairs={{0,1},{1,0},{2,3},{3,2},{4,5},{5,4},{6,7},{7,6},{8,9},{9,8},{10,11... | collective-permute-start | bytes 589832 | tf_op jit(solution)/shard_map/ppermute | solution.py:31
  121.6 13.8 %collective-permute-start.37 = (bf16[32,3072]{1,0:T(8,128)(2,1)}, bf16[32,3072]{1,0:T(8,128)(2,1)}, u32[]{:S(2)}, u32[]{:S(2)}) collective-permute-start(bf16[32,3072]{1,0:T(8,128)(2,1)} %collective-permute-done.33.refs_1_.refs_5_), channel_id=1, source_target_pairs={{0,6},{2,0},{4,2},{6,4},{1,7},{3,1},{5,3},{7,5},{8,14},{10,8},{12,... | collective-permute-start | bytes 589832 | tf_op jit(solution)/shard_map/ppermute | solution.py:31
  160.0 13.0 %collective-permute-start.46 = (f32[2,3072]{1,0:T(2,128)S(1)}, f32[2,3072]{1,0:T(2,128)S(1)}, u32[]{:S(2)}, u32[]{:S(2)}) collective-permute-start(f32[2,3072]{1,0:T(2,128)S(1)} %add.139), channel_id=1, source_target_pairs={{0,4},{2,6},{4,0},{6,2},{1,5},{3,7},{5,1},{7,3},{8,12},{10,14},{12... | collective-permute-start | bytes 73736 | tf_op jit(solution)/shard_map/ppermute | solution.py:84
  160.5 12.5 %collective-permute-start.47 = (f32[2,3072]{1,0:T(2,128)S(1)}, f32[2,3072]{1,0:T(2,128)S(1)}, u32[]{:S(2)}, u32[]{:S(2)}) collective-permute-start(f32[2,3072]{1,0:T(2,128)S(1)} %add.139), channel_id=1, source_target_pairs={{0,6},{2,4},{4,2},{6,0},{1,7},{3,5},{5,3},{7,1},{8,14},{10,12},{12... | collective-permute-start | bytes 73736 | tf_op jit(solution)/shard_map/ppermute | solution.py:84
  161.8 11.3 %collective-permute-start.45 = (f32[2,3072]{1,0:T(2,128)S(1)}, f32[2,3072]{1,0:T(2,128)S(1)}, u32[]{:S(2)}, u32[]{:S(2)}) collective-permute-start(f32[2,3072]{1,0:T(2,128)S(1)} %add.139), channel_id=1, source_target_pairs={{0,2},{2,0},{4,6},{6,4},{1,3},{3,1},{5,7},{7,5},{8,10},{10,8},{12,... | collective-permute-start | bytes 73736 | tf_op jit(solution)/shard_map/ppermute | solution.py:84
  193.7 10.7 %collective-permute-start.60 = (bf16[32,3072]{1,0:T(8,128)(2,1)S(1)}, bf16[32,3072]{1,0:T(8,128)(2,1)S(1)}, u32[]{:S(2)}, u32[]{:S(2)}) collective-permute-start(bf16[32,3072]{1,0:T(8,128)(2,1)S(1)} %add_convert_fusion.2), channel_id=1, source_target_pairs={{0,6},{2,0},{4,2},{6,4},{1,7},{3,1},{5,3},{7,5},{8,14},{10,8},{12,... | collective-permute-start | bytes 589832 | tf_op jit(solution)/shard_map/ppermute | solution.py:31
  224.3 9.9 %collective-permute-start.65 = (bf16[32,3072]{1,0:T(8,128)(2,1)S(1)}, bf16[32,3072]{1,0:T(8,128)(2,1)S(1)}, u32[]{:S(2)}, u32[]{:S(2)}) collective-permute-start(bf16[32,3072]{1,0:T(8,128)(2,1)S(1)} %collective-permute-done.63.refs_1_), channel_id=1, source_target_pairs={{0,1},{1,0},{2,3},{3,2},{4,5},{5,4},{6,7},{7,6},{8,9},{9,8},{10,11... | collective-permute-start | bytes 589832 | tf_op jit(solution)/shard_map/ppermute | solution.py:31
  225.6 11.8 %collective-permute-start.67 = (bf16[32,3072]{1,0:T(8,128)(2,1)S(1)}, bf16[32,3072]{1,0:T(8,128)(2,1)S(1)}, u32[]{:S(2)}, u32[]{:S(2)}) collective-permute-start(bf16[32,3072]{1,0:T(8,128)(2,1)S(1)} %collective-permute-done.63.refs_1_), channel_id=1, source_target_pairs={{0,6},{2,0},{4,2},{6,4},{1,7},{3,1},{5,3},{7,5},{8,14},{10,8},{12,... | collective-permute-start | bytes 589832 | tf_op jit(solution)/shard_map/ppermute | solution.py:31
  233.3 13.8 %collective-permute-start.68 = (bf16[32,3072]{1,0:T(8,128)(2,1)S(1)}, bf16[32,3072]{1,0:T(8,128)(2,1)S(1)}, u32[]{:S(2)}, u32[]{:S(2)}) collective-permute-start(bf16[32,3072]{1,0:T(8,128)(2,1)S(1)} %collective-permute-done.66.refs_0_.refs_4_), channel_id=1, source_target_pairs={{0,1},{1,0},{2,3},{3,2},{4,5},{5,4},{6,7},{7,6},{8,9},{9,8},{10,11... | collective-permute-start | bytes 589832 | tf_op jit(solution)/shard_map/ppermute | solution.py:31
  234.1 13.0 %collective-permute-start.70 = (bf16[32,3072]{1,0:T(8,128)(2,1)S(1)}, bf16[32,3072]{1,0:T(8,128)(2,1)S(1)}, u32[]{:S(2)}, u32[]{:S(2)}) collective-permute-start(bf16[32,3072]{1,0:T(8,128)(2,1)S(1)} %collective-permute-done.66.refs_0_.refs_4_), channel_id=1, source_target_pairs={{0,2},{2,4},{4,6},{6,0},{1,3},{3,5},{5,7},{7,1},{8,10},{10,12},{12... | collective-permute-start | bytes 589832 | tf_op jit(solution)/shard_map/ppermute | solution.py:31
  237.5 11.8 %collective-permute-start.69 = (bf16[32,3072]{1,0:T(8,128)(2,1)S(1)}, bf16[32,3072]{1,0:T(8,128)(2,1)S(1)}, u32[]{:S(2)}, u32[]{:S(2)}) collective-permute-start(bf16[32,3072]{1,0:T(8,128)(2,1)S(1)} %collective-permute-done.67.refs_1_.refs_5_), channel_id=1, source_target_pairs={{0,1},{1,0},{2,3},{3,2},{4,5},{5,4},{6,7},{7,6},{8,9},{9,8},{10,11... | collective-permute-start | bytes 589832 | tf_op jit(solution)/shard_map/ppermute | solution.py:31
  238.2 11.1 %collective-permute-start.71 = (bf16[32,3072]{1,0:T(8,128)(2,1)S(1)}, bf16[32,3072]{1,0:T(8,128)(2,1)S(1)}, u32[]{:S(2)}, u32[]{:S(2)}) collective-permute-start(bf16[32,3072]{1,0:T(8,128)(2,1)S(1)} %collective-permute-done.67.refs_1_.refs_5_), channel_id=1, source_target_pairs={{0,6},{2,0},{4,2},{6,4},{1,7},{3,1},{5,3},{7,5},{8,14},{10,8},{12,... | collective-permute-start | bytes 589832 | tf_op jit(solution)/shard_map/ppermute | solution.py:31
  247.1 13.7 %collective-permute-start.72 = (bf16[32,3072]{1,0:T(8,128)(2,1)S(1)}, bf16[32,3072]{1,0:T(8,128)(2,1)S(1)}, u32[]{:S(2)}, u32[]{:S(2)}) collective-permute-start(bf16[32,3072]{1,0:T(8,128)(2,1)S(1)} %collective-permute-done.70.refs_0_.refs_8_), channel_id=1, source_target_pairs={{0,1},{1,0},{2,3},{3,2},{4,5},{5,4},{6,7},{7,6},{8,9},{9,8},{10,11... | collective-permute-start | bytes 589832 | tf_op jit(solution)/shard_map/ppermute | solution.py:31
  247.9 13.6 %collective-permute-start.74 = (bf16[32,3072]{1,0:T(8,128)(2,1)S(1)}, bf16[32,3072]{1,0:T(8,128)(2,1)}, u32[]{:S(2)}, u32[]{:S(2)}) collective-permute-start(bf16[32,3072]{1,0:T(8,128)(2,1)S(1)} %collective-permute-done.70.refs_0_.refs_8_), channel_id=1, source_target_pairs={{0,2},{2,4},{4,6},{6,0},{1,3},{3,5},{5,7},{7,1},{8,10},{10,12},{12... | collective-permute-start | bytes 589832 | tf_op jit(solution)/shard_map/ppermute | solution.py:31
  249.3 13.0 %collective-permute-start.73 = (bf16[32,3072]{1,0:T(8,128)(2,1)S(1)}, bf16[32,3072]{1,0:T(8,128)(2,1)S(1)}, u32[]{:S(2)}, u32[]{:S(2)}) collective-permute-start(bf16[32,3072]{1,0:T(8,128)(2,1)S(1)} %collective-permute-done.71.refs_1_.refs_9_), channel_id=1, source_target_pairs={{0,1},{1,0},{2,3},{3,2},{4,5},{5,4},{6,7},{7,6},{8,9},{9,8},{10,11... | collective-permute-start | bytes 589832 | tf_op jit(solution)/shard_map/ppermute | solution.py:31
  250.1 12.9 %collective-permute-start.75 = (bf16[32,3072]{1,0:T(8,128)(2,1)S(1)}, bf16[32,3072]{1,0:T(8,128)(2,1)}, u32[]{:S(2)}, u32[]{:S(2)}) collective-permute-start(bf16[32,3072]{1,0:T(8,128)(2,1)S(1)} %collective-permute-done.71.refs_1_.refs_9_), channel_id=1, source_target_pairs={{0,6},{2,0},{4,2},{6,4},{1,7},{3,1},{5,3},{7,5},{8,14},{10,8},{12,... | collective-permute-start | bytes 589832 | tf_op jit(solution)/shard_map/ppermute | solution.py:31
  261.5 21.2 %collective-permute-start.76 = (bf16[32,3072]{1,0:T(8,128)(2,1)}, bf16[32,3072]{1,0:T(8,128)(2,1)}, u32[]{:S(2)}, u32[]{:S(2)}) collective-permute-start(bf16[32,3072]{1,0:T(8,128)(2,1)} %collective-permute-done.74.refs_0_.refs_12_), channel_id=1, source_target_pairs={{0,1},{1,0},{2,3},{3,2},{4,5},{5,4},{6,7},{7,6},{8,9},{9,8},{10,11... | collective-permute-start | bytes 589832 | tf_op jit(solution)/shard_map/ppermute | solution.py:31
  263.0 19.7 %collective-permute-start.77 = (bf16[32,3072]{1,0:T(8,128)(2,1)}, bf16[32,3072]{1,0:T(8,128)(2,1)}, u32[]{:S(2)}, u32[]{:S(2)}) collective-permute-start(bf16[32,3072]{1,0:T(8,128)(2,1)} %collective-permute-done.75.refs_1_.refs_13_), channel_id=1, source_target_pairs={{0,1},{1,0},{2,3},{3,2},{4,5},{5,4},{6,7},{7,6},{8,9},{9,8},{10,11... | collective-permute-start | bytes 589832 | tf_op jit(solution)/shard_map/ppermute | solution.py:31
  (181 other events, 1955.2 us)

commit v2 on v1

--- a/solution.py
+++ b/solution.py
@@ -17,6 +17,7 @@
 F32 = jnp.float32
 BF16 = jnp.bfloat16
 VMEM_SPEC = pl.BlockSpec(memory_space=pltpu.VMEM)
+HBM_SPEC = pl.BlockSpec(memory_space=pltpu.HBM)
 SMEM_SPEC = pl.BlockSpec(memory_space=pltpu.SMEM)
 
 
@@ -66,16 +67,16 @@
     for s in list(range(1, depth)) + [0]:
         terms = slab_pieces(s)
         for h in range(HALVES):
-            total = terms[h].astype(F32)
+            parts = [terms[h]]
             for j in range(1, width):
                 piece = terms[j * HALVES + h]
                 if last[j][h] is not None:
                     piece = after(piece, last[j][h])
                 last[j][h] = shift(piece, "tensor", -j)
-                total = total + last[j][h].astype(F32)
+                parts.append(last[j][h])
             if running[h] is not None:
-                total = total + shift(running[h], "dp", way(h)).astype(F32)
-            running[h] = total if s == 0 else total.astype(BF16)
+                parts.append(shift(running[h], "dp", way(h)))
+            running[h] = parts if s == 0 else sum(part.astype(F32) for part in parts).astype(BF16)
     return running
 
 
@@ -123,13 +124,15 @@
     return jnp.dot(left, right, preferred_element_type=F32)
 
 
-def call(kernel, out_shape, ins, specs=None, scratch=(), flops=0, moved=1000000, limit=24):
+def call(
+    kernel, out_shape, ins, specs=None, outs=None, scratch=(), flops=0, moved=1000000, limit=16
+):
     many = isinstance(out_shape, (tuple, list))
     return pl.pallas_call(
         kernel,
         out_shape=out_shape,
         in_specs=specs or [VMEM_SPEC] * len(ins),
-        out_specs=[VMEM_SPEC] * len(out_shape) if many else VMEM_SPEC,
+        out_specs=outs or ([VMEM_SPEC] * len(out_shape) if many else VMEM_SPEC),
         scratch_shapes=list(scratch),
         compiler_params=pltpu.CompilerParams(vmem_limit_bytes=limit * 2**20),
         cost_estimate=pl.CostEstimate(flops=flops, bytes_accessed=moved, transcendentals=0),
@@ -168,6 +171,14 @@
             out[:, ring : ring + count, :] = held[:, pl.ds(first, count), :].astype(out.dtype)
         else:
             out[ring : ring + count, :] = held[pl.ds(first, count), :].astype(out.dtype)
+
+
+def to_joined_order(held, out, pieces):
+    lane_count = held.shape[2]
+    for ring, first, count in pieces:
+        for t in range(held.shape[0]):
+            part = held[t, pl.ds(first, count), :].astype(out.dtype)
+            out[ring : ring + count, t * lane_count : (t + 1) * lane_count] = part
 
 
 def head_forward(held, gains, rows, lanes):
@@ -215,15 +226,9 @@
 
 def attend_margin_kernel(local_count, depth, width, *refs):
     slabs = refs[:depth]
-    gain_ref, out_weight_ref, select_ref = refs[depth : depth + 3]
-    rows = refs[depth + 3 : depth + 3 + HALVES]
-    sums_ref, pooled_ref, held = refs[depth + 3 + HALVES :]
-    select = select_ref[...]
-    rows_own = jnp.concatenate([ref[...] for ref in rows], axis=0).astype(F32)
-    for image in range(select.shape[1]):
-        pooled_ref[image : image + 1, :] = jnp.sum(
-            rows_own * select[:, image : image + 1], axis=0, keepdims=True
-        )
+    gain_ref, out_weight_ref = refs[depth : depth + 2]
+    row_sums = refs[depth + 2 : depth + 2 + HALVES]
+    sums_ref, pooled_ref, held = refs[depth + 2 + HALVES :]
     pieces = piece_rows(local_count, depth, width)
     to_section_order(slabs, held, pieces)
     gains = gain_ref[...]
@@ -237,7 +242,7 @@
     middle = rest.astype(BF16)
     low = (rest - middle.astype(F32)).astype(BF16)
     weights = out_weight_ref[...]
-    pooled_ref[...] = pooled_ref[...] + (
+    pooled_ref[...] = sum(ref[...] for ref in row_sums) + (
         dot(high, weights) + (dot(middle, weights) + dot(low, weights))
     )
 
@@ -291,19 +296,19 @@
                 gains[t : t + 1, :],
             )
         held[2, rows, lanes] = dot(turned_ref[place], grad_mixed)
-    to_ring_order(held, out_ref, pieces)
+    to_joined_order(held, out_ref, pieces)
 
 
 def project_kernel(*refs):
-    weights_ref, projected_ref = refs[-2:]
-    rows = jnp.concatenate([ref[...] for ref in refs[:-2]], axis=0)
+    *pieces, weights_ref, projected_ref = refs
+    rows = jnp.concatenate([ref[...] for ref in pieces], axis=0)
     for t in range(weights_ref.shape[0]):
         projected_ref[t, :, :] = dot(rows, weights_ref[t])
 
 
 def cotangent_kernel(*refs):
-    weights_ref, out_ref = refs[-2:]
-    rows = jnp.concatenate([ref[...] for ref in refs[:-2]], axis=0)
+    *pieces, weights_ref, out_ref = refs
+    rows = jnp.concatenate([ref[...] for ref in pieces], axis=0)
     out_ref[...] = dot_nt(rows, weights_ref[...])
 
 
@@ -318,34 +323,59 @@
 
 
 def input_kernel(first, count, gradient_ref, weights_ref, *outs):
-    rows = slice(first, first + count)
-    total = dot_nt(gradient_ref[0, rows, :], weights_ref[0])
-    for t in range(1, weights_ref.shape[0]):
-        total = total + dot_nt(gradient_ref[t, rows, :], weights_ref[t])
+    projections, _, lane_count = weights_ref.shape
+    total = None
+    for t in range(projections):
+        part = gradient_ref[first : first + count, t * lane_count : (t + 1) * lane_count]
+        part = dot_nt(part, weights_ref[t])
+        total = part if total is None else total + part
     to_pieces(total, outs)
 
 
-def weight_gradient_kernel(count, first, *refs):
-    pieces, gradient_ref, added, out_ref = refs[:count], refs[count], refs[count + 1 : -1], refs[-1]
-    rows = jnp.concatenate([ref[...] for ref in pieces], axis=0)
-    for t in range(out_ref.shape[0]):
-        total = dot_tn(rows, gradient_ref[first + t])
-        if added:
-            total = total + added[t][0].astype(F32)
-        out_ref[t, :, :] = total.astype(BF16)
-
-
-def out_gradient_kernel(*refs):
-    attention_ref, sums_ref, grad_image_ref, out_ref = refs[-4:]
-    cotangent = jnp.concatenate([ref[...] for ref in refs[:-4]], axis=0)
-    total = dot_tn(attention_ref[...], cotangent)
+def weight_gradient_kernel(counts, chunk, *refs):
+    pieces, grads = refs[: sum(counts)], refs[sum(counts) : -2]
+    out_ref, joined = refs[-2:]
+    projections, model_width, lane_count = out_ref.shape
+    first = 0
+    for grad in grads:
+        joined[first : first + grad.shape[0], :] = grad[...]
+        first += grad.shape[0]
+
+    def step(*blocks):
+        rows = jnp.concatenate([block[...] for block in blocks[:-1]], axis=0)
+        total = dot_tn(rows, joined[...]).astype(BF16)
+        for t in range(projections):
+            blocks[-1][t, :, :] = total[:, t * lane_count : (t + 1) * lane_count]
+
+    pltpu.emit_pipeline(
+        step,
+        grid=(model_width // chunk,),
+        in_specs=[pl.BlockSpec((p.shape[0], chunk), lambda i: (0, i)) for p in pieces],
+        out_specs=[pl.BlockSpec((projections, chunk, lane_count), lambda i: (0, i, 0))],
+    )(*pieces, out_ref)
+
+
+def out_gradient_kernel(chunk, *refs):
+    *pieces, attention_ref, sums_ref, grad_image_ref, out_ref = refs
     sums = sums_ref[...]
     image_count, lane_count = sums.shape
     sums = jnp.concatenate([sums, jnp.zeros((-image_count % 8, lane_count), F32)], axis=0).T
-    grad_image = grad_image_ref[...].astype(BF16).astype(F32)
-    for image in range(image_count):
-        total = total + sums[:, image : image + 1] * grad_image[image : image + 1, :]
-    out_ref[...] = total.astype(BF16)
+
+    def step(*blocks):
+        cotangent = jnp.concatenate([block[...] for block in blocks[:-2]], axis=0)
+        total = dot_tn(attention_ref[...], cotangent)
+        grad_image = blocks[-2][...].astype(BF16).astype(F32)
+        for image in range(image_count):
+            total = total + sums[:, image : image + 1] * grad_image[image : image + 1, :]
+        blocks[-1][...] = total.astype(BF16)
+
+    pltpu.emit_pipeline(
+        step,
+        grid=(out_ref.shape[1] // chunk,),
+        in_specs=[pl.BlockSpec((p.shape[0], chunk), lambda i: (0, i)) for p in pieces]
+        + [pl.BlockSpec((image_count, chunk), lambda i: (0, i))],
+        out_specs=[pl.BlockSpec((lane_count, chunk), lambda i: (0, i))],
+    )(*pieces, grad_image_ref, out_ref)
 
 
 def head_gradient_kernel(width, pooled_half_ref, grad_logits_ref, out_ref):
@@ -366,23 +396,32 @@
     refs[-1][...] = jnp.concatenate([ref[...] for ref in refs[:-1]], axis=0)
 
 
-def norm_rows_kernel(rows_ref, gain_ref, out_ref):
-    unit_rows, _ = norm_parts(rows_ref[...].astype(F32))
+def norm_rows_kernel(first, rows_ref, gain_ref, out_ref):
+    rows = rows_ref[first : first + out_ref.shape[0], :].astype(F32)
+    unit_rows, _ = norm_parts(rows)
     out_ref[...] = (unit_rows * gain_ref[...]).astype(BF16)
 
 
-def norm_margin_kernel(first_ref, rows_ref, received_ref, gain_ref, out_ref, margin_ref):
-    first = first_ref[0] == 1
-
-    @pl.when(first)
-    def _():
-        margin_ref[...] = rows_ref[...]
-
-    @pl.when(jnp.logical_not(first))
-    def _():
-        margin_ref[...] = received_ref[...]
-
-    norm_rows_kernel(margin_ref, gain_ref, out_ref)
+def norm_margin_kernel(
+    first, flag_ref, rows_ref, received_ref, select_ref, gain_ref, out_ref, margin_ref, sums_ref
+):
+    own = rows_ref[first : first + out_ref.shape[0], :]
+    margin = jnp.where(flag_ref[0] == 1, own.astype(F32), received_ref[...].astype(F32))
+    margin_ref[...] = margin.astype(BF16)
+    unit_rows, _ = norm_parts(margin)
+    out_ref[...] = (unit_rows * gain_ref[...]).astype(BF16)
+    select = select_ref[...]
+    for image in range(select.shape[1]):
+        sums_ref[image : image + 1, :] = jnp.sum(
+            margin * select[:, image : image + 1], axis=0, keepdims=True
+        )
+
+
+def out_rows_kernel(first, rows_ref, *refs):
+    *terms, out_ref = refs
+    total = sum(term[...].astype(F32) for term in terms)
+    rows = rows_ref[first : first + out_ref.shape[0], :].astype(F32)
+    out_ref[...] = (rows + total).astype(BF16)
 
 
 def judge_kernel(
@@ -422,9 +461,11 @@
     per_image_ref[...] = dot_nt(grad_image.astype(BF16), out_weight_ref[...])
 
 
-def grad_rows_kernel(grad_ref, rows_ref, select_ref, grad_image_ref, gain_ref, out_ref):
+def grad_rows_kernel(rows_ref, select_ref, grad_image_ref, gain_ref, *refs):
+    *terms, out_ref = refs
     unit_rows, inverse = norm_parts(rows_ref[...].astype(F32))
-    total = norm_back(grad_ref[...], unit_rows, inverse, gain_ref[...])
+    grad = sum(term[...].astype(F32) for term in terms)
+    total = norm_back(grad, unit_rows, inverse, gain_ref[...])
     select = select_ref[...]
     for image in range(grad_image_ref.shape[0]):
         total = total + select[:, image : image + 1] * grad_image_ref[image : image + 1, :]
@@ -464,8 +505,7 @@
     chunk = 2 * PATCHES if model_width % (2 * PATCHES) == 0 else PATCHES
     piece_shapes = [half_shape] * (width * HALVES)
 
-    def halves_of(rows):
-        return [rows[h * half : (h + 1) * half] for h in range(HALVES)]
+    select_halves = [own_select[h * half : (h + 1) * half] for h in range(HALVES)]
 
     def project(_, pieces):
         return call(
@@ -473,7 +513,7 @@
             shape((3, slab_rows, lane_count)),
             (*pieces, qkv_local),
             flops=3 * slab_flops,
-            limit=16,
+            limit=12,
         )
 
     def state_of(projected):
@@ -491,28 +531,15 @@
             flops=2 * product_flops,
         )
 
-    def weight_gradient(slabs, gradient, first, count, *added):
-        pieces = [piece for slab in slabs for piece in slab]
-        return pl.pallas_call(
-            functools.partial(weight_gradient_kernel, len(pieces), first),
-            grid=(model_width // chunk,),
-            out_shape=shape((count, model_width, lane_count), BF16),
-            in_specs=[pl.BlockSpec((half, chunk), lambda i: (0, i))] * len(pieces)
-            + [pl.BlockSpec(three, lambda i: (0, 0, 0))]
-            + [pl.BlockSpec((1, chunk, lane_count), lambda i: (0, i, 0))] * len(added),
-            out_specs=pl.BlockSpec((count, chunk, lane_count), lambda i: (0, i, 0)),
-            compiler_params=pltpu.CompilerParams(vmem_limit_bytes=20 * 2**20),
-            cost_estimate=pl.CostEstimate(
-                flops=count * depth * slab_flops,
-                bytes_accessed=4 * count * model_width * lane_count,
-                transcendentals=0,
-            ),
-        )(*pieces, gradient, *added)
-
     own_slabs, own_projected = gather_slabs(
         [
-            call(norm_rows_kernel, half_shape, (rows, norm_gain), limit=4)
-            for rows in halves_of(rows_in)
+            call(
+                functools.partial(norm_rows_kernel, h * half),
+                half_shape,
+                (rows_in, norm_gain),
+                limit=4,
+            )
+            for h in range(HALVES)
         ],
         project,
     )
@@ -530,38 +557,42 @@
             piece_shapes,
             (attention, out_local),
             flops=slab_flops,
-            limit=16,
+            limit=12,
         )
 
     out_halves = [
-        (rows.astype(F32) + total).astype(BF16)
-        for rows, total in zip(halves_of(rows_in), scatter_slabs(branch))
+        call(
+            functools.partial(out_rows_kernel, h * half),
+            half_shape,
+            (rows_in, *terms),
+            limit=4,
+        )
+        for h, terms in enumerate(scatter_slabs(branch))
     ]
 
     first = (lax.axis_index("section") == 0).astype(jnp.int32).reshape(1)
-    margin_normed, margin_halves = zip(
+    margin_normed, margin_halves, row_sums = zip(
         *[
             call(
-                norm_margin_kernel,
-                [half_shape] * 2,
-                (first, rows, from_behind(out, "section", 1), norm_gain),
-                specs=[SMEM_SPEC] + [VMEM_SPEC] * 3,
+                functools.partial(norm_margin_kernel, h * half),
+                [half_shape, half_shape, shape((image_count, model_width))],
+                (first, rows_in, from_behind(out, "section", 1), select, norm_gain),
+                specs=[SMEM_SPEC] + [VMEM_SPEC] * 4,
                 limit=4,
             )
-            for rows, out in zip(halves_of(rows_in), out_halves)
+            for h, (out, select) in enumerate(zip(out_halves, select_halves))
         ]
     )
     margin_slabs, margin_projected = gather_slabs(margin_normed, project)
     image_sums, pooled_part = call(
         functools.partial(attend_margin_kernel, *place),
         [shape((image_count, lane_count)), shape((image_count, model_width))],
-        (*margin_projected, gain_pair, out_local, own_select, *margin_halves),
+        (*margin_projected, gain_pair, out_local, *row_sums),
         scratch=[pltpu.VMEM(three, F32)],
         flops=2 * product_flops,
     )
-    own_state = state_of(own_projected)
     margin_state = state_of(margin_projected)
-    pooled = after(sum_group(pooled_part), own_state[4], margin_state[4])
+    pooled = after(sum_group(pooled_part), margin_state[4])
     losses, pooled_half, grad_logits, grad_image, per_image = call(
         functools.partial(judge_kernel, PATCHES),
         [
@@ -574,7 +605,7 @@
         (pooled, pool_gain, class_head[0], label_row, out_local),
         specs=[VMEM_SPEC] * 3 + [SMEM_SPEC, VMEM_SPEC],
         flops=4 * class_count * model_width * 8,
-        limit=16,
+        limit=12,
     )
     grad_head = call(
         functools.partial(head_gradient_kernel, width),
@@ -585,7 +616,7 @@
 
     margin_gradient = call(
         functools.partial(attend_back_kernel, *place, True),
-        shape(three, BF16),
+        shape((row_count, 3 * lane_count), BF16),
         (*margin_state, per_image, gain_pair),
         scratch=[pltpu.VMEM(three, F32)],
         flops=5 * product_flops,
@@ -597,58 +628,63 @@
             piece_shapes,
             (margin_gradient, qkv_local),
             flops=3 * slab_flops,
-            limit=16,
+            limit=12,
         )
 
     grad_normed = scatter_slabs(input_term)
     grad_inputs = [
-        call(grad_rows_kernel, half_shape, (grad, rows, select, grad_image, norm_gain), limit=6)
-        for grad, rows, select in zip(grad_normed, margin_halves, halves_of(own_select))
+        call(
+            grad_rows_kernel,
+            half_shape,
+            (rows, select, grad_image, norm_gain, *terms),
+            limit=6,
+        )
+        for terms, rows, select in zip(grad_normed, margin_halves, select_halves)
     ]
-    margin_parts = [weight_gradient(margin_slabs, margin_gradient, t, 1) for t in range(3)]
-
     returned = [from_behind(grad, "section", -1) for grad in grad_inputs]
 
-    def cotangent(s, pieces):
-        if s < len(margin_parts):
-            pieces = [after(pieces[0], margin_parts[s])] + pieces[1:]
+    def cotangent(_, pieces):
         return call(
             cotangent_kernel,
             shape((slab_rows, lane_count)),
             (*pieces, out_local),
             flops=slab_flops,
-            limit=16,
+            limit=12,
         )
 
     cotangent_slabs, grad_attention = gather_slabs(returned, cotangent)
     own_gradient = call(
         functools.partial(attend_back_kernel, *place, False),
-        shape(three, BF16),
-        (*own_state, *grad_attention, gain_pair),
+        shape((row_count, 3 * lane_count), BF16),
+        (*state_of(own_projected), *grad_attention, gain_pair),
         scratch=[pltpu.VMEM(three, F32), pltpu.VMEM(three[1:], F32)],
         flops=5 * product_flops,
     )
-    query_key_value_gradient = weight_gradient(own_slabs, own_gradient, 0, 3, *margin_parts)
+    passes = [[p for slab in slabs for p in slab] for slabs in (margin_slabs, own_slabs)]
+    counts = [len(pieces) for pieces in passes]
+    query_key_value_gradient = call(
+        functools.partial(weight_gradient_kernel, counts, chunk),
+        shape((3, model_width, lane_count), BF16),
+        (*passes[0], *passes[1], margin_gradient, own_gradient),
+        specs=[HBM_SPEC] * sum(counts) + [VMEM_SPEC] * 2,
+        outs=HBM_SPEC,
+        scratch=[pltpu.VMEM((2 * row_count, 3 * lane_count), BF16)],
+        flops=6 * depth * slab_flops,
+        moved=6 * model_width * lane_count,
+        limit=60,
+    )
     pieces = [piece for slab in cotangent_slabs for piece in slab]
     wide = 2 * chunk if model_width % (2 * chunk) == 0 else chunk
-    grad_out = pl.pallas_call(
-        out_gradient_kernel,
-        grid=(model_width // wide,),
-        out_shape=shape((lane_count, model_width), BF16),
-        in_specs=[pl.BlockSpec((half, wide), lambda i: (0, i))] * len(pieces)
-        + [
-            pl.BlockSpec((row_count, lane_count), lambda i: (0, 0)),
-            pl.BlockSpec((image_count, lane_count), lambda i: (0, 0)),
-            pl.BlockSpec((image_count, wide), lambda i: (0, i)),
-        ],
-        out_specs=pl.BlockSpec((lane_count, wide), lambda i: (0, i)),
-        compiler_params=pltpu.CompilerParams(vmem_limit_bytes=20 * 2**20),
-        cost_estimate=pl.CostEstimate(
-            flops=depth * slab_flops,
-            bytes_accessed=4 * model_width * lane_count,
-            transcendentals=0,
-        ),
-    )(*pieces, attention, image_sums, grad_image)
+    grad_out = call(
+        functools.partial(out_gradient_kernel, wide),
+        shape((lane_count, model_width), BF16),
+        (*pieces, attention, image_sums, grad_image),
+        specs=[HBM_SPEC] * len(pieces) + [VMEM_SPEC] * 2 + [HBM_SPEC],
+        outs=HBM_SPEC,
+        flops=depth * slab_flops,
+        moved=4 * model_width * lane_count,
+        limit=60,
+    )
     out_own = call(join_kernel, shape((local_count, model_width), BF16), tuple(out_halves), limit=4)
     return (
         out_own[None],

time: 307 us -> 295 us (0.961)
  the two profiles are of different devices: /device:TPU:0 before, /device:TPU:2 now
where the time goes in v2:
time: 295 us; the launch traced here: 293 us
  starting transfers between devices  119 us (40%)
  waiting for transfers between devices  77.7 us (26%)
  Pallas kernels  72.2 us (24%)
  local copies, waits for them, and re-layouts  20.2 us (7%)
    ppermute x70, starting transfers between devices, shift(): lax.ppermute(block, axis, [(i, (i + distance) % count) for i in range(cou...  104 us
    pallas_call x39, Pallas kernels, call(): pl.pallas_call(kernel, out_shape=out_shape, in_specs=specs or [VMEM_SPEC]...  72.2 us
    ppermute x70, waiting for transfers between devices, shift(): lax.ppermute(block, axis, [(i, (i + distance) % count) for i in range(cou...  70 us
    unnamed x172, local copies, waits for them, and re-layouts  20.2 us
    ppermute x4, starting transfers between devices, from_behind(): return lax.ppermute(block, axis, route)  8.93 us
  transfers between devices with their start and end apart: 78, of which 40 were waited for; matrix products, arithmetic and copies ran while one was open for 1% of the time, Pallas kernels for 10%

profile of v2, /device:TPU:2, one launch (start us, length us, event | category | flops | bytes accessed | tf_op | source)
XLA Modules:
  0.0 293.0 jit_solution(3557302234988515421)
XLA Ops:
  8.9 3.4 %collective-permute-done.2.refs_0_.refs_20_ = bf16[32,3072]{1,0:T(8,128)(2,1)S(1)} collective-permute-done((bf16[32,3072]{1,0:T(8,128)(2,1)S(1)}, bf16[32,3072]{1,0:T(8,128)(2,1)S(1)}, u32[]{:S(2)}, u32[]{:S(2)}) %collective-permute-start.2) | collective-permute-done | bytes 196640 | tf_op jit(solution)/shard_map/ppermute | solution.py:32
  19.7 3.0 %copy-done = bf16[1,3,3072,384]{3,2,1,0:T(8,128)(2,1)S(1)} copy-done((bf16[1,3,3072,384]{3,2,1,0:T(8,128)(2,1)S(1)}, bf16[1,3,3072,384]{3,2,1,0:T(8,128)(2,1)}, u32[]{:S(2)}) %copy-start) | copy-done | bytes 7077912
  24.8 3.8 %collective-permute-start.11 = (bf16[32,3072]{1,0:T(8,128)(2,1)S(1)}, bf16[32,3072]{1,0:T(8,128)(2,1)S(1)}, u32[]{:S(2)}, u32[]{:S(2)}) collective-permute-start(bf16[32,3072]{1,0:T(8,128)(2,1)S(1)} %collective-permute-done.7.refs_1_.refs_25_), channel_id=1, source_target_pairs={{0,6},{2,0},{4,2},{6,4},{1,7},{3,1},{5,3},{7,5},{8,14},{10,8},{12,... | collective-permute-start | bytes 589832 | tf_op jit(solution)/shard_map/ppermute | solution.py:32
  36.7 3.0 %copy-done.2 = bf16[1,3,3072,384]{3,2,1,0:T(8,128)(2,1)S(1)} copy-done((bf16[1,3,3072,384]{3,2,1,0:T(8,128)(2,1)S(1)}, bf16[1,3,3072,384]{3,2,1,0:T(8,128)(2,1)}, u32[]{:S(2)}) %copy-start.2) | copy-done | bytes 7077912
  52.1 4.0 %collective-permute-done.21 = bf16[32,3072]{1,0:T(8,128)(2,1)S(1)} collective-permute-done((bf16[32,3072]{1,0:T(8,128)(2,1)S(1)}, bf16[32,3072]{1,0:T(8,128)(2,1)S(1)}, u32[]{:S(2)}, u32[]{:S(2)}) %collective-permute-start.21) | collective-permute-done | bytes 196640 | tf_op jit(solution)/shard_map/ppermute | solution.py:32
  58.0 2.3 collective-permute-done.14
  64.6 12.8 %collective-permute-start.26 = (bf16[32,3072]{1,0:T(8,128)(2,1)S(1)}, bf16[32,3072]{1,0:T(8,128)(2,1)S(1)}, u32[]{:S(2)}, u32[]{:S(2)}) collective-permute-start(bf16[32,3072]{1,0:T(8,128)(2,1)S(1)} %add_convert_fusion.7), channel_id=1, source_target_pairs={{0,6},{2,0},{4,2},{6,4},{1,7},{3,1},{5,3},{7,5},{8,14},{10,8},{12,... | collective-permute-start | bytes 589832 | tf_op jit(solution)/shard_map/ppermute | solution.py:32
  80.4 7.6 %collective-permute-done.26 = bf16[32,3072]{1,0:T(8,128)(2,1)S(1)} collective-permute-done((bf16[32,3072]{1,0:T(8,128)(2,1)S(1)}, bf16[32,3072]{1,0:T(8,128)(2,1)S(1)}, u32[]{:S(2)}, u32[]{:S(2)}) %collective-permute-start.26) | collective-permute-done | bytes 196640 | tf_op jit(solution)/shard_map/ppermute | solution.py:32
  92.4 3.5 %collective-permute-done.27.refs_2_ = bf16[32,3072]{1,0:T(8,128)(2,1)S(1)} collective-permute-done((bf16[32,3072]{1,0:T(8,128)(2,1)S(1)}, bf16[32,3072]{1,0:T(8,128)(2,1)S(1)}, u32[]{:S(2)}, u32[]{:S(2)}) %collective-permute-start.27) | collective-permute-done | bytes 196640 | tf_op jit(solution)/shard_map/ppermute | solution.py:32
  100.1 5.1 %collective-permute-done.28.received_ref = bf16[32,3072]{1,0:T(8,128)(2,1)S(1)} collective-permute-done((bf16[32,3072]{1,0:T(8,128)(2,1)S(1)}, bf16[32,3072]{1,0:T(8,128)(2,1)S(1)}, u32[]{:S(2)}, u32[]{:S(2)}) %collective-permute-start.28) | collective-permute-done | bytes 196640 | tf_op jit(solution)/shard_map/ppermute | solution.py:27
  107.1 3.6 %collective-permute-start.33 = (bf16[32,3072]{1,0:T(8,128)(2,1)S(1)}, bf16[32,3072]{1,0:T(8,128)(2,1)S(1)}, u32[]{:S(2)}, u32[]{:S(2)}) collective-permute-start(bf16[32,3072]{1,0:T(8,128)(2,1)S(1)} %get-tuple-element.120.refs_1_), channel_id=1, source_target_pairs={{0,6},{2,0},{4,2},{6,4},{1,7},{3,1},{5,3},{7,5},{8,14},{10,8},{12,... | collective-permute-start | bytes 589832 | tf_op jit(solution)/shard_map/ppermute | solution.py:32
  114.6 3.4 %collective-permute-done.33.refs_1_.refs_5_ = bf16[32,3072]{1,0:T(8,128)(2,1)S(1)} collective-permute-done((bf16[32,3072]{1,0:T(8,128)(2,1)S(1)}, bf16[32,3072]{1,0:T(8,128)(2,1)S(1)}, u32[]{:S(2)}, u32[]{:S(2)}) %collective-permute-start.33) | collective-permute-done | bytes 196640 | tf_op jit(solution)/shard_map/ppermute | solution.py:32
  126.5 3.1 %collective-permute-start.41 = (bf16[32,3072]{1,0:T(8,128)(2,1)S(1)}, bf16[32,3072]{1,0:T(8,128)(2,1)S(1)}, u32[]{:S(2)}, u32[]{:S(2)}) collective-permute-start(bf16[32,3072]{1,0:T(8,128)(2,1)S(1)} %collective-permute-done.37.refs_1_.refs_9_), channel_id=1, source_target_pairs={{0,6},{2,0},{4,2},{6,4},{1,7},{3,1},{5,3},{7,5},{8,14},{10,8},{12,... | collective-permute-start | bytes 589832 | tf_op jit(solution)/shard_map/ppermute | solution.py:32
  133.2 3.4 %collective-permute-done.39.refs_3_.refs_11_ = bf16[32,3072]{1,0:T(8,128)(2,1)S(1)} collective-permute-done((bf16[32,3072]{1,0:T(8,128)(2,1)S(1)}, bf16[32,3072]{1,0:T(8,128)(2,1)S(1)}, u32[]{:S(2)}, u32[]{:S(2)}) %collective-permute-start.39) | collective-permute-done | bytes 196640 | tf_op jit(solution)/shard_map/ppermute | solution.py:32
  139.3 3.0 %collective-permute-done.43.refs_3_.refs_15_ = bf16[32,3072]{1,0:T(8,128)(2,1)S(1)} collective-permute-done((bf16[32,3072]{1,0:T(8,128)(2,1)S(1)}, bf16[32,3072]{1,0:T(8,128)(2,1)S(1)}, u32[]{:S(2)}, u32[]{:S(2)}) %collective-permute-start.43) | collective-permute-done | bytes 196640 | tf_op jit(solution)/shard_map/ppermute | solution.py:32
  143.8 2.7 shard_map.140
  147.8 2.7 collective-permute-done.44
  152.2 2.8 collective-permute-start.45
  154.9 2.7 shard_map.139
  157.7 3.3 %shard_map.141 = (f32[2,1]{1,0:T(2,128)S(1)}, bf16[2,3072]{1,0:T(2,128)(2,1)S(1)}, bf16[2,512]{1,0:T(2,128)(2,1)S(1)}, f32[2,3072]{1,0:T(2,128)S(1)}, f32[2,384]{1,0:T(2,128)S(1)}) custom-call(f32[2,3072]{1,0:T(2,128)S(1)} %add_add_fusion.pooled_ref, f32[1,3072]{1,0:T(1,128)S(1)} %copy-done.78, bf16[3072,512]{1,0:T(8,128)(2,1)S(1)} %bitcast.42, ...), custom_call_target="tpu_custom_call" | custom-call | flops 50331648 | bytes 1000000 | tf_op jit(solution)/shard_map/pallas_call | solution.py:131
  161.0 3.2 %shard_map.142.gradient_ref.refs_32_ = bf16[512,1152]{1,0:T(8,128)(2,1)S(1)} custom-call(f32[6,256,256]{2,1,0:T(8,128)S(1)} %get-tuple-element.127.refs_0_, bf16[6,256,256]{2,1,0:T(8,128)(2,1)S(1)} %get-tuple-element.128.refs_1_, bf16[3,512,384]{2,1,0:T(8,128)(2,1)S(1)} %get-tuple-element.129.refs_2_, f32[2,512,384]{2,1,0:T(8,128)S(1)} %get-tuple-element.130.refs_3_, ...), custom_call_target="tpu_custom_call" | custom-call | flops 503316480 | bytes 1000000 | tf_op jit(solution)/shard_map/pallas_call | solution.py:131
  180.0 2.3 collective-permute-done.60
  203.3 2.6 collective-permute-done.54.refs_2_
  206.5 3.2 %collective-permute-start.55 = (bf16[32,3072]{1,0:T(8,128)(2,1)S(1)}, bf16[32,3072]{1,0:T(8,128)(2,1)S(1)}, u32[]{:S(2)}, u32[]{:S(2)}) collective-permute-start(bf16[32,3072]{1,0:T(8,128)(2,1)S(1)} %shard_map.148), channel_id=1, source_target_pairs={{8,0},{16,8},{24,16},{9,1},{17,9},{25,17},{10,2},{18,10},{26,18},{... | collective-permute-start | bytes 589832 | tf_op jit(solution)/shard_map/ppermute | solution.py:27
  209.7 2.5 collective-permute-start.67
  213.5 3.5 %collective-permute-start.66 = (bf16[32,3072]{1,0:T(8,128)(2,1)S(1)}, bf16[32,3072]{1,0:T(8,128)(2,1)S(1)}, u32[]{:S(2)}, u32[]{:S(2)}) collective-permute-start(bf16[32,3072]{1,0:T(8,128)(2,1)S(1)} %collective-permute-done.55.refs_0_), channel_id=1, source_target_pairs={{0,2},{2,4},{4,6},{6,0},{1,3},{3,5},{5,7},{7,1},{8,10},{10,12},{12... | collective-permute-start | bytes 589832 | tf_op jit(solution)/shard_map/ppermute | solution.py:32
  224.7 3.7 %collective-permute-start.70 = (bf16[32,3072]{1,0:T(8,128)(2,1)S(1)}, bf16[32,3072]{1,0:T(8,128)(2,1)S(1)}, u32[]{:S(2)}, u32[]{:S(2)}) collective-permute-start(bf16[32,3072]{1,0:T(8,128)(2,1)S(1)} %collective-permute-done.66.refs_0_.refs_4_), channel_id=1, source_target_pairs={{0,2},{2,4},{4,6},{6,0},{1,3},{3,5},{5,7},{7,1},{8,10},{10,12},{12... | collective-permute-start | bytes 589832 | tf_op jit(solution)/shard_map/ppermute | solution.py:32
  230.1 6.6 %collective-permute-done.71.refs_1_.refs_9_ = bf16[32,3072]{1,0:T(8,128)(2,1)S(1)} collective-permute-done((bf16[32,3072]{1,0:T(8,128)(2,1)S(1)}, bf16[32,3072]{1,0:T(8,128)(2,1)S(1)}, u32[]{:S(2)}, u32[]{:S(2)}) %collective-permute-start.71) | collective-permute-done | bytes 196640 | tf_op jit(solution)/shard_map/ppermute | solution.py:32
  250.9 2.7 shard_map.143
  267.7 2.9 shard_map.154.refs_33_
  271.6 6.1 %shard_map.156 = bf16[384,3072]{1,0:T(8,128)(2,1)} custom-call(bf16[32,3072]{1,0:T(8,128)(2,1)} %copy-done.19, bf16[32,3072]{1,0:T(8,128)(2,1)} %copy-done.18, bf16[32,3072]{1,0:T(8,128)(2,1)} %copy-done.23, bf16[32,3072]{1,0:T(8,128)(2,1)} %copy-done.21, bf16[32,3072]{1,0:T(8,128)(2,1)} %copy-done.22, bf16[32,3072]{1,0:T(8,128)(2,1)} %copy-done.20, ...), custom_call_target="tpu_custom_call" | custom-call | flops 1207959552 | bytes 4718592 | tf_op jit(solution)/shard_map/pallas_call | solution.py:131
  277.7 15.1 %shard_map.155 = bf16[3,3072,384]{2,1,0:T(8,128)(2,1)} custom-call(bf16[32,3072]{1,0:T(8,128)(2,1)} %copy-done.61, bf16[32,3072]{1,0:T(8,128)(2,1)} %copy-done.64, bf16[32,3072]{1,0:T(8,128)(2,1)} %copy-done.63, bf16[32,3072]{1,0:T(8,128)(2,1)} %copy-done.66, bf16[32,3072]{1,0:T(8,128)(2,1)} %copy-done.62, bf16[32,3072]{1,0:T(8,128)(2,1)} %copy-done.65, ...), custom_call_target="tpu_custom_call" | custom-call | flops 7247757312 | bytes 7077888 | tf_op jit(solution)/shard_map/pallas_call | solution.py:131
  (354 shorter events, 157.5 us)
Async XLA Ops:
  2.6 9.6 %collective-permute-start.2 = (bf16[32,3072]{1,0:T(8,128)(2,1)S(1)}, bf16[32,3072]{1,0:T(8,128)(2,1)S(1)}, u32[]{:S(2)}, u32[]{:S(2)}) collective-permute-start(bf16[32,3072]{1,0:T(8,128)(2,1)S(1)} %shard_map.119.refs_0_.refs_16_), channel_id=1, source_target_pairs={{0,2},{2,4},{4,6},{6,0},{1,3},{3,5},{5,7},{7,1},{8,10},{10,12},{12... | collective-permute-start | bytes 589832 | tf_op jit(solution)/shard_map/ppermute | solution.py:32
  6.0 10.0 %collective-permute-start.3 = (bf16[32,3072]{1,0:T(8,128)(2,1)S(1)}, bf16[32,3072]{1,0:T(8,128)(2,1)S(1)}, u32[]{:S(2)}, u32[]{:S(2)}) collective-permute-start(bf16[32,3072]{1,0:T(8,128)(2,1)S(1)} %shard_map.120.refs_1_.refs_17_), channel_id=1, source_target_pairs={{0,6},{2,0},{4,2},{6,4},{1,7},{3,1},{5,3},{7,5},{8,14},{10,8},{12,... | collective-permute-start | bytes 589832 | tf_op jit(solution)/shard_map/ppermute | solution.py:32
  12.3 11.9 %collective-permute-start.6 = (bf16[32,3072]{1,0:T(8,128)(2,1)S(1)}, bf16[32,3072]{1,0:T(8,128)(2,1)S(1)}, u32[]{:S(2)}, u32[]{:S(2)}) collective-permute-start(bf16[32,3072]{1,0:T(8,128)(2,1)S(1)} %collective-permute-done.2.refs_0_.refs_20_), channel_id=1, source_target_pairs={{0,2},{2,4},{4,6},{6,0},{1,3},{3,5},{5,7},{7,1},{8,10},{10,12},{12... | collective-permute-start | bytes 589832 | tf_op jit(solution)/shard_map/ppermute | solution.py:32
  13.7 10.5 %collective-permute-start.4 = (bf16[32,3072]{1,0:T(8,128)(2,1)S(1)}, bf16[32,3072]{1,0:T(8,128)(2,1)S(1)}, u32[]{:S(2)}, u32[]{:S(2)}) collective-permute-start(bf16[32,3072]{1,0:T(8,128)(2,1)S(1)} %collective-permute-done.2.refs_0_.refs_20_), channel_id=1, source_target_pairs={{0,1},{1,0},{2,3},{3,2},{4,5},{5,4},{6,7},{7,6},{8,9},{9,8},{10,11... | collective-permute-start | bytes 589832 | tf_op jit(solution)/shard_map/ppermute | solution.py:32
  16.2 8.6 %collective-permute-start.7 = (bf16[32,3072]{1,0:T(8,128)(2,1)S(1)}, bf16[32,3072]{1,0:T(8,128)(2,1)S(1)}, u32[]{:S(2)}, u32[]{:S(2)}) collective-permute-start(bf16[32,3072]{1,0:T(8,128)(2,1)S(1)} %collective-permute-done.3.refs_1_.refs_21_), channel_id=1, source_target_pairs={{0,6},{2,0},{4,2},{6,4},{1,7},{3,1},{5,3},{7,5},{8,14},{10,8},{12,... | collective-permute-start | bytes 589832 | tf_op jit(solution)/shard_map/ppermute | solution.py:32
  24.2 8.8 %collective-permute-start.8 = (bf16[32,3072]{1,0:T(8,128)(2,1)S(1)}, bf16[32,3072]{1,0:T(8,128)(2,1)S(1)}, u32[]{:S(2)}, u32[]{:S(2)}) collective-permute-start(bf16[32,3072]{1,0:T(8,128)(2,1)S(1)} %collective-permute-done.6.refs_0_.refs_24_), channel_id=1, source_target_pairs={{0,1},{1,0},{2,3},{3,2},{4,5},{5,4},{6,7},{7,6},{8,9},{9,8},{10,11... | collective-permute-start | bytes 589832 | tf_op jit(solution)/shard_map/ppermute | solution.py:32
  24.8 10.1 %collective-permute-start.11 = (bf16[32,3072]{1,0:T(8,128)(2,1)S(1)}, bf16[32,3072]{1,0:T(8,128)(2,1)S(1)}, u32[]{:S(2)}, u32[]{:S(2)}) collective-permute-start(bf16[32,3072]{1,0:T(8,128)(2,1)S(1)} %collective-permute-done.7.refs_1_.refs_25_), channel_id=1, source_target_pairs={{0,6},{2,0},{4,2},{6,4},{1,7},{3,1},{5,3},{7,5},{8,14},{10,8},{12,... | collective-permute-start | bytes 589832 | tf_op jit(solution)/shard_map/ppermute | solution.py:32
  49.5 10.8 %collective-permute-start.14 = (bf16[32,3072]{1,0:T(8,128)(2,1)S(1)}, bf16[32,3072]{1,0:T(8,128)(2,1)S(1)}, u32[]{:S(2)}, u32[]{:S(2)}) collective-permute-start(bf16[32,3072]{1,0:T(8,128)(2,1)S(1)} %get-tuple-element.101), channel_id=1, source_target_pairs={{0,1},{1,0},{2,3},{3,2},{4,5},{5,4},{6,7},{7,6},{8,9},{9,8},{10,11... | collective-permute-start | bytes 589832 | tf_op jit(solution)/shard_map/ppermute | solution.py:32
  60.4 17.6 %collective-permute-start.18 = (bf16[32,3072]{1,0:T(8,128)(2,1)S(1)}, bf16[32,3072]{1,0:T(8,128)(2,1)S(1)}, u32[]{:S(2)}, u32[]{:S(2)}) collective-permute-start(bf16[32,3072]{1,0:T(8,128)(2,1)S(1)} %add_convert_fusion.11), channel_id=1, source_target_pairs={{0,2},{2,4},{4,6},{6,0},{1,3},{3,5},{5,7},{7,1},{8,10},{10,12},{12... | collective-permute-start | bytes 589832 | tf_op jit(solution)/shard_map/ppermute | solution.py:32
  60.4 17.6 %collective-permute-start.15 = (bf16[32,3072]{1,0:T(8,128)(2,1)S(1)}, bf16[32,3072]{1,0:T(8,128)(2,1)S(1)}, u32[]{:S(2)}, u32[]{:S(2)}) collective-permute-start(bf16[32,3072]{1,0:T(8,128)(2,1)S(1)} %get-tuple-element.102), channel_id=1, source_target_pairs={{0,1},{1,0},{2,3},{3,2},{4,5},{5,4},{6,7},{7,6},{8,9},{9,8},{10,11... | collective-permute-start | bytes 589832 | tf_op jit(solution)/shard_map/ppermute | solution.py:32
  64.6 23.4 %collective-permute-start.26 = (bf16[32,3072]{1,0:T(8,128)(2,1)S(1)}, bf16[32,3072]{1,0:T(8,128)(2,1)S(1)}, u32[]{:S(2)}, u32[]{:S(2)}) collective-permute-start(bf16[32,3072]{1,0:T(8,128)(2,1)S(1)} %add_convert_fusion.7), channel_id=1, source_target_pairs={{0,6},{2,0},{4,2},{6,4},{1,7},{3,1},{5,3},{7,5},{8,14},{10,8},{12,... | collective-permute-start | bytes 589832 | tf_op jit(solution)/shard_map/ppermute | solution.py:32
  77.3 10.6 %collective-permute-start.23 = (bf16[32,3072]{1,0:T(8,128)(2,1)S(1)}, bf16[32,3072]{1,0:T(8,128)(2,1)S(1)}, u32[]{:S(2)}, u32[]{:S(2)}) collective-permute-start(bf16[32,3072]{1,0:T(8,128)(2,1)S(1)} %get-tuple-element.114), channel_id=1, source_target_pairs={{0,1},{1,0},{2,3},{3,2},{4,5},{5,4},{6,7},{7,6},{8,9},{9,8},{10,11... | collective-permute-start | bytes 589832 | tf_op jit(solution)/shard_map/ppermute | solution.py:32
  78.1 10.0 %collective-permute-start.19 = (bf16[32,3072]{1,0:T(8,128)(2,1)S(1)}, bf16[32,3072]{1,0:T(8,128)(2,1)S(1)}, u32[]{:S(2)}, u32[]{:S(2)}) collective-permute-start(bf16[32,3072]{1,0:T(8,128)(2,1)S(1)} %add_convert_fusion.10), channel_id=1, source_target_pairs={{0,2},{2,4},{4,6},{6,0},{1,3},{3,5},{5,7},{7,1},{8,10},{10,12},{12... | collective-permute-start | bytes 589832 | tf_op jit(solution)/shard_map/ppermute | solution.py:32
  79.3 8.8 %collective-permute-start.16 = (bf16[32,3072]{1,0:T(8,128)(2,1)S(1)}, bf16[32,3072]{1,0:T(8,128)(2,1)S(1)}, u32[]{:S(2)}, u32[]{:S(2)}) collective-permute-start(bf16[32,3072]{1,0:T(8,128)(2,1)S(1)} %get-tuple-element.103), channel_id=1, source_target_pairs={{0,1},{1,0},{2,3},{3,2},{4,5},{5,4},{6,7},{7,6},{8,9},{9,8},{10,11... | collective-permute-start | bytes 589832 | tf_op jit(solution)/shard_map/ppermute | solution.py:32
  88.2 9.8 %collective-permute-start.20 = (bf16[32,3072]{1,0:T(8,128)(2,1)S(1)}, bf16[32,3072]{1,0:T(8,128)(2,1)S(1)}, u32[]{:S(2)}, u32[]{:S(2)}) collective-permute-start(bf16[32,3072]{1,0:T(8,128)(2,1)S(1)} %add_convert_fusion.9), channel_id=1, source_target_pairs={{0,2},{2,4},{4,6},{6,0},{1,3},{3,5},{5,7},{7,1},{8,10},{10,12},{12... | collective-permute-start | bytes 589832 | tf_op jit(solution)/shard_map/ppermute | solution.py:32
  96.1 10.7 %collective-permute-start.29 = (bf16[32,3072]{1,0:T(8,128)(2,1)S(1)}, bf16[32,3072]{1,0:T(8,128)(2,1)S(1)}, u32[]{:S(2)}, u32[]{:S(2)}) collective-permute-start(bf16[32,3072]{1,0:T(8,128)(2,1)S(1)} %shard_map.131.refs_1_), channel_id=1, source_target_pairs={{0,8},{8,16},{16,24},{1,9},{9,17},{17,25},{2,10},{10,18},{18,26},{... | collective-permute-start | bytes 589832 | tf_op jit(solution)/shard_map/ppermute | solution.py:27
  107.1 10.9 %collective-permute-start.33 = (bf16[32,3072]{1,0:T(8,128)(2,1)S(1)}, bf16[32,3072]{1,0:T(8,128)(2,1)S(1)}, u32[]{:S(2)}, u32[]{:S(2)}) collective-permute-start(bf16[32,3072]{1,0:T(8,128)(2,1)S(1)} %get-tuple-element.120.refs_1_), channel_id=1, source_target_pairs={{0,6},{2,0},{4,2},{6,4},{1,7},{3,1},{5,3},{7,5},{8,14},{10,8},{12,... | collective-permute-start | bytes 589832 | tf_op jit(solution)/shard_map/ppermute | solution.py:32
  118.0 8.5 %collective-permute-start.37 = (bf16[32,3072]{1,0:T(8,128)(2,1)S(1)}, bf16[32,3072]{1,0:T(8,128)(2,1)S(1)}, u32[]{:S(2)}, u32[]{:S(2)}) collective-permute-start(bf16[32,3072]{1,0:T(8,128)(2,1)S(1)} %collective-permute-done.33.refs_1_.refs_5_), channel_id=1, source_target_pairs={{0,6},{2,0},{4,2},{6,4},{1,7},{3,1},{5,3},{7,5},{8,14},{10,8},{12,... | collective-permute-start | bytes 589832 | tf_op jit(solution)/shard_map/ppermute | solution.py:32
  122.2 9.4 %collective-permute-start.38 = (bf16[32,3072]{1,0:T(8,128)(2,1)S(1)}, bf16[32,3072]{1,0:T(8,128)(2,1)S(1)}, u32[]{:S(2)}, u32[]{:S(2)}) collective-permute-start(bf16[32,3072]{1,0:T(8,128)(2,1)S(1)} %collective-permute-done.36.refs_0_.refs_8_), channel_id=1, source_target_pairs={{0,1},{1,0},{2,3},{3,2},{4,5},{5,4},{6,7},{7,6},{8,9},{9,8},{10,11... | collective-permute-start | bytes 589832 | tf_op jit(solution)/shard_map/ppermute | solution.py:32
  166.6 9.1 %collective-permute-start.56 = (bf16[32,3072]{1,0:T(8,128)(2,1)S(1)}, bf16[32,3072]{1,0:T(8,128)(2,1)S(1)}, u32[]{:S(2)}, u32[]{:S(2)}) collective-permute-start(bf16[32,3072]{1,0:T(8,128)(2,1)S(1)} %get-tuple-element.160), channel_id=1, source_target_pairs={{0,1},{1,0},{2,3},{3,2},{4,5},{5,4},{6,7},{7,6},{8,9},{9,8},{10,11... | collective-permute-start | bytes 589832 | tf_op jit(solution)/shard_map/ppermute | solution.py:32
  178.4 9.6 %collective-permute-start.52 = (bf16[32,3072]{1,0:T(8,128)(2,1)S(1)}, bf16[32,3072]{1,0:T(8,128)(2,1)S(1)}, u32[]{:S(2)}, u32[]{:S(2)}) collective-permute-start(bf16[32,3072]{1,0:T(8,128)(2,1)S(1)} %add_convert_fusion.5), channel_id=1, source_target_pairs={{0,2},{2,4},{4,6},{6,0},{1,3},{3,5},{5,7},{7,1},{8,10},{10,12},{12... | collective-permute-start | bytes 589832 | tf_op jit(solution)/shard_map/ppermute | solution.py:32
  179.0 9.5 %collective-permute-start.49 = (bf16[32,3072]{1,0:T(8,128)(2,1)S(1)}, bf16[32,3072]{1,0:T(8,128)(2,1)S(1)}, u32[]{:S(2)}, u32[]{:S(2)}) collective-permute-start(bf16[32,3072]{1,0:T(8,128)(2,1)S(1)} %get-tuple-element.149), channel_id=1, source_target_pairs={{0,1},{1,0},{2,3},{3,2},{4,5},{5,4},{6,7},{7,6},{8,9},{9,8},{10,11... | collective-permute-start | bytes 589832 | tf_op jit(solution)/shard_map/ppermute | solution.py:32
  188.6 9.8 %collective-permute-start.53 = (bf16[32,3072]{1,0:T(8,128)(2,1)S(1)}, bf16[32,3072]{1,0:T(8,128)(2,1)S(1)}, u32[]{:S(2)}, u32[]{:S(2)}) collective-permute-start(bf16[32,3072]{1,0:T(8,128)(2,1)S(1)} %add_convert_fusion.4), channel_id=1, source_target_pairs={{0,2},{2,4},{4,6},{6,0},{1,3},{3,5},{5,7},{7,1},{8,10},{10,12},{12... | collective-permute-start | bytes 589832 | tf_op jit(solution)/shard_map/ppermute | solution.py:32
  189.1 9.3 %collective-permute-start.50 = (bf16[32,3072]{1,0:T(8,128)(2,1)S(1)}, bf16[32,3072]{1,0:T(8,128)(2,1)S(1)}, u32[]{:S(2)}, u32[]{:S(2)}) collective-permute-start(bf16[32,3072]{1,0:T(8,128)(2,1)S(1)} %get-tuple-element.150), channel_id=1, source_target_pairs={{0,1},{1,0},{2,3},{3,2},{4,5},{5,4},{6,7},{7,6},{8,9},{9,8},{10,11... | collective-permute-start | bytes 589832 | tf_op jit(solution)/shard_map/ppermute | solution.py:32
  209.7 10.5 %collective-permute-start.67 = (bf16[32,3072]{1,0:T(8,128)(2,1)S(1)}, bf16[32,3072]{1,0:T(8,128)(2,1)S(1)}, u32[]{:S(2)}, u32[]{:S(2)}) collective-permute-start(bf16[32,3072]{1,0:T(8,128)(2,1)S(1)} %collective-permute-done.63.refs_1_), channel_id=1, source_target_pairs={{0,6},{2,0},{4,2},{6,4},{1,7},{3,1},{5,3},{7,5},{8,14},{10,8},{12,... | collective-permute-start | bytes 589832 | tf_op jit(solution)/shard_map/ppermute | solution.py:32
  213.5 11.1 %collective-permute-start.66 = (bf16[32,3072]{1,0:T(8,128)(2,1)S(1)}, bf16[32,3072]{1,0:T(8,128)(2,1)S(1)}, u32[]{:S(2)}, u32[]{:S(2)}) collective-permute-start(bf16[32,3072]{1,0:T(8,128)(2,1)S(1)} %collective-permute-done.55.refs_0_), channel_id=1, source_target_pairs={{0,2},{2,4},{4,6},{6,0},{1,3},{3,5},{5,7},{7,1},{8,10},{10,12},{12... | collective-permute-start | bytes 589832 | tf_op jit(solution)/shard_map/ppermute | solution.py:32
  220.2 16.5 %collective-permute-start.71 = (bf16[32,3072]{1,0:T(8,128)(2,1)S(1)}, bf16[32,3072]{1,0:T(8,128)(2,1)S(1)}, u32[]{:S(2)}, u32[]{:S(2)}) collective-permute-start(bf16[32,3072]{1,0:T(8,128)(2,1)S(1)} %collective-permute-done.67.refs_1_.refs_5_), channel_id=1, source_target_pairs={{0,6},{2,0},{4,2},{6,4},{1,7},{3,1},{5,3},{7,5},{8,14},{10,8},{12,... | collective-permute-start | bytes 589832 | tf_op jit(solution)/shard_map/ppermute | solution.py:32
  222.4 14.3 %collective-permute-start.69 = (bf16[32,3072]{1,0:T(8,128)(2,1)S(1)}, bf16[32,3072]{1,0:T(8,128)(2,1)S(1)}, u32[]{:S(2)}, u32[]{:S(2)}) collective-permute-start(bf16[32,3072]{1,0:T(8,128)(2,1)S(1)} %collective-permute-done.67.refs_1_.refs_5_), channel_id=1, source_target_pairs={{0,1},{1,0},{2,3},{3,2},{4,5},{5,4},{6,7},{7,6},{8,9},{9,8},{10,11... | collective-permute-start | bytes 589832 | tf_op jit(solution)/shard_map/ppermute | solution.py:32
  224.7 13.6 %collective-permute-start.70 = (bf16[32,3072]{1,0:T(8,128)(2,1)S(1)}, bf16[32,3072]{1,0:T(8,128)(2,1)S(1)}, u32[]{:S(2)}, u32[]{:S(2)}) collective-permute-start(bf16[32,3072]{1,0:T(8,128)(2,1)S(1)} %collective-permute-done.66.refs_0_.refs_4_), channel_id=1, source_target_pairs={{0,2},{2,4},{4,6},{6,0},{1,3},{3,5},{5,7},{7,1},{8,10},{10,12},{12... | collective-permute-start | bytes 589832 | tf_op jit(solution)/shard_map/ppermute | solution.py:32
  228.4 9.9 %collective-permute-start.68 = (bf16[32,3072]{1,0:T(8,128)(2,1)S(1)}, bf16[32,3072]{1,0:T(8,128)(2,1)S(1)}, u32[]{:S(2)}, u32[]{:S(2)}) collective-permute-start(bf16[32,3072]{1,0:T(8,128)(2,1)S(1)} %collective-permute-done.66.refs_0_.refs_4_), channel_id=1, source_target_pairs={{0,1},{1,0},{2,3},{3,2},{4,5},{5,4},{6,7},{7,6},{8,9},{9,8},{10,11... | collective-permute-start | bytes 589832 | tf_op jit(solution)/shard_map/ppermute | solution.py:32
  245.1 20.3 %collective-permute-start.77 = (bf16[32,3072]{1,0:T(8,128)(2,1)}, bf16[32,3072]{1,0:T(8,128)(2,1)}, u32[]{:S(2)}, u32[]{:S(2)}) collective-permute-start(bf16[32,3072]{1,0:T(8,128)(2,1)} %collective-permute-done.75.refs_1_.refs_13_), channel_id=1, source_target_pairs={{0,1},{1,0},{2,3},{3,2},{4,5},{5,4},{6,7},{7,6},{8,9},{9,8},{10,11... | collective-permute-start | bytes 589832 | tf_op jit(solution)/shard_map/ppermute | solution.py:32
  249.3 16.1 %collective-permute-start.76 = (bf16[32,3072]{1,0:T(8,128)(2,1)}, bf16[32,3072]{1,0:T(8,128)(2,1)}, u32[]{:S(2)}, u32[]{:S(2)}) collective-permute-start(bf16[32,3072]{1,0:T(8,128)(2,1)} %collective-permute-done.74.refs_0_.refs_12_), channel_id=1, source_target_pairs={{0,1},{1,0},{2,3},{3,2},{4,5},{5,4},{6,7},{7,6},{8,9},{9,8},{10,11... | collective-permute-start | bytes 589832 | tf_op jit(solution)/shard_map/ppermute | solution.py:32
  (132 other events, 1196.5 us)
